TPU v7x, 32 devices: a whole 2x2x4 slice. The times are simulated.
32 devices in a mesh: leaf: 16 (over z, x, core), rhs: 2 (over y).
Axes of the slice: x: 2, y: 2, z: 4, core: 2. Of those that a mesh axis runs over, the one named last changes fastest.
Arguments:
- vectors: bfloat16 [64, 65536], P('rhs', 'leaf'), may hold values from -6 to 6
- leaf_basis: bfloat16 [1024, 64, 64], P('leaf'), may hold values from -0.75 to 0.75
- local_transfer: bfloat16 [2032, 64, 64], P('leaf'), may hold values from -0.5 to 0.5
- coupling: bfloat16 [2032, 4, 64, 64], P('leaf'), may hold values from -0.375 to 0.375
- coupling_source: int32 [2032, 4], P('leaf'), may hold values from 0 to 1023, as said below
- top_transfer: bfloat16 [14, 64, 64], replicated, may hold values from -0.5 to 0.5
- top_coupling: bfloat16 [64, 64, 64], P('leaf'), may hold values from -0.75 to 0.75
- top_target: int32 [64], P('leaf'), may hold values from 2 to 15, as said below
- top_source: int32 [64], P('leaf'), may hold values from 2 to 15, as said below
- near_blocks: bfloat16 [1024, 8, 64, 64], P('leaf', 'rhs'), may hold values from -0.25 to 0.25
- near_source: int32 [1024, 8], P('leaf', 'rhs'), may hold values from 0 to 1023, as said below
Outputs:
- product: bfloat16 [64, 65536], P('rhs', 'leaf')
Inputs may be any that keep to these rules, and one draw needn't show every extreme that they name: `coupling_source`: entry k of a row names a node of that row's level other than the row's own node, at most n away from it along the level, where n is the level's nodes of one subtree; entry 0 is the node's sibling. near_source[t, 0] is t; every other entry of row t lies within 64 leaves of t and differs from t. `top_target`: an upper heap node; top_target[b] and top_source[b] are different nodes of the same upper level. `top_source`: an upper heap node of the same level as top_target[b], never equal to it.
All inputs are finite; a program needn't handle non-finite values.
Results may differ from a plain program's by a relative error of at most 0.025.
Values may be sent and summed in bfloat16 or wider, within the bound.
A program may use at most 128 MiB of HBM per device.

v0:
```python
import jax
import jax.numpy as jnp
from jax import lax
from jax.sharding import PartitionSpec as P

full_precision = lax.Precision.HIGHEST


def padded(array, sides, width):
    for axis, dim in sides:
        size, length = (lax.axis_size(axis), array.shape[dim])
        up = [(i, (i + 1) % size) for i in range(size - 1)]
        down = [(j, i) for i, j in up]
        last = lax.slice_in_dim(array, length - width, length, axis=dim)
        initial = lax.slice_in_dim(array, 0, width, axis=dim)
        before = lax.ppermute(last, axis, up)
        after = lax.ppermute(initial, axis, down)
        array = jnp.concatenate([before, array, after], axis=dim)
    return array


def level_table(leaf_count):
    layout = []
    first_node = 0
    node_count = leaf_count
    while node_count >= 1:
        layout.append((first_node, node_count))
        first_node += node_count
        node_count //= 2
    return layout


def descend(upper_field, top_transfer, root_count):
    upper_down = upper_field[:, 2:4]
    level_size = 4
    while level_size < root_count:
        parents = jnp.repeat(upper_down, 2, axis=1)
        transfer_rows = top_transfer[level_size - 2 : 2 * level_size - 2].astype(jnp.float32)
        upper_down = upper_field[:, level_size : 2 * level_size] + jnp.einsum(
            "rhb,hab->rha", parents, transfer_rows, precision=full_precision
        )
        level_size *= 2
    return upper_down


def shards(
    vectors,
    leaf_basis,
    local_transfer,
    coupling,
    coupling_source,
    top_transfer,
    top_coupling,
    top_target,
    top_source,
    near_blocks,
    near_source,
):
    rhs_local = vectors.shape[0]
    leaf_count = leaf_basis.shape[0]
    leaf_size = leaf_basis.shape[1]
    rank_size = leaf_basis.shape[2]
    slot_count = coupling.shape[1]
    node_total = coupling.shape[0]
    layout = level_table(leaf_count)
    root_count = lax.axis_size("leaf")
    my_index = lax.axis_index("leaf")
    leaf_points = vectors.reshape(rhs_local, leaf_count, leaf_size)
    coefficients = [
        jnp.einsum(
            "rip,ipk->rik", leaf_points, leaf_basis, preferred_element_type=jnp.float32
        ).astype(jnp.bfloat16)
    ]
    for height in range(1, len(layout)):
        first_node, node_count = layout[height - 1]
        lifted = jnp.einsum(
            "rik,ikm->rim",
            coefficients[-1],
            local_transfer[first_node : first_node + node_count],
            preferred_element_type=jnp.float32,
        )
        coefficients.append(
            lifted.reshape(rhs_local, node_count // 2, 2, rank_size)
            .sum(axis=2)
            .astype(jnp.bfloat16)
        )
    fields = []
    for height in range(len(layout)):
        node_count = layout[height][1]
        extended = padded(coefficients[height], (("leaf", 1),), node_count)
        couple_first_node, couple_node_count = layout[height]
        source_ids = (
            coupling_source[couple_first_node : couple_first_node + couple_node_count]
            - (my_index - 1) * couple_node_count
        )
        picked = jnp.take(extended, source_ids.reshape(-1), axis=1).reshape(
            rhs_local, couple_node_count, slot_count, rank_size
        )
        fields.append(
            jnp.einsum(
                "rtkm,tkmn->rtn",
                picked,
                coupling[couple_first_node : couple_first_node + couple_node_count],
                preferred_element_type=jnp.float32,
            )
        )
    root_row = node_total - 1
    root_transfer = local_transfer[root_row : root_row + 1]
    root_term = jnp.einsum(
        "rdk,dkm->rdm", coefficients[-1], root_transfer, preferred_element_type=jnp.float32
    )
    root_terms = lax.all_gather(root_term, "leaf", axis=1, tiled=True)
    upper = [
        root_terms.reshape(rhs_local, root_count // 2, 2, rank_size)
        .sum(axis=2)
        .astype(jnp.bfloat16)
    ]
    level_size = root_count // 2
    while level_size > 2:
        lifted = jnp.einsum(
            "rhk,hkm->rhm",
            upper[0],
            top_transfer[level_size - 2 : 2 * level_size - 2],
            preferred_element_type=jnp.float32,
        )
        upper.insert(
            0,
            lifted.reshape(rhs_local, level_size // 2, 2, rank_size)
            .sum(axis=2)
            .astype(jnp.bfloat16),
        )
        level_size //= 2
    heap_coef = jnp.concatenate(
        [jnp.zeros((rhs_local, 2, rank_size), jnp.bfloat16)] + upper, axis=1
    )
    sources_up = jnp.take(heap_coef, top_source, axis=1)
    contrib = jnp.einsum(
        "rbm,bmn->rbn", sources_up, top_coupling, preferred_element_type=jnp.float32
    )
    onehot_targets = (
        top_target[:, None] == jnp.arange(root_count, dtype=jnp.int32)[None, :]
    ).astype(jnp.float32)
    partial_field = jnp.einsum("rbn,bh->rhn", contrib, onehot_targets, precision=full_precision)
    upper_field = lax.psum(partial_field, "leaf")
    upper_down = descend(upper_field, top_transfer, root_count)
    parent_down = lax.dynamic_slice_in_dim(upper_down, my_index // 2, 1, axis=1)
    descent = (
        fields[-1]
        + jnp.einsum(
            "rdb,dab->rda", parent_down, root_transfer.astype(jnp.float32), precision=full_precision
        )
    ).astype(jnp.bfloat16)
    for height in range(len(layout) - 2, -1, -1):
        first_node, node_count = layout[height]
        parents = jnp.repeat(descent, 2, axis=1)
        descent = (
            fields[height]
            + jnp.einsum(
                "rtb,tab->rta",
                parents,
                local_transfer[first_node : first_node + node_count],
                preferred_element_type=jnp.float32,
            )
        ).astype(jnp.bfloat16)
    far_part = jnp.einsum("rik,ipk->rip", descent, leaf_basis, preferred_element_type=jnp.float32)
    all_columns = lax.all_gather(vectors, "rhs", axis=0, tiled=True)
    points = padded(all_columns, (("leaf", 1),), vectors.shape[1])
    leaves_seen = points.reshape(points.shape[0], -1, leaf_size)
    positions = near_source - (my_index - 1) * leaf_count
    gathered = jnp.take(leaves_seen, positions.reshape(-1), axis=1).reshape(
        points.shape[0], leaf_count, near_source.shape[1], leaf_size
    )
    near_sum = lax.psum_scatter(
        jnp.einsum("rijq,ijpq->rip", gathered, near_blocks, preferred_element_type=jnp.float32),
        "rhs",
        scatter_dimension=0,
        tiled=True,
    )
    return (far_part + near_sum).reshape(rhs_local, -1).astype(jnp.bfloat16)


def solution(mesh):
    placed = (
        P("rhs", "leaf"),
        P("leaf", None, None),
        P("leaf", None, None),
        P("leaf", None, None, None),
        P("leaf", None),
        P(),
        P("leaf", None, None),
        P("leaf"),
        P("leaf"),
        P("leaf", "rhs", None, None),
        P("leaf", "rhs"),
    )
    return jax.shard_map(
        shards, mesh=mesh, in_specs=placed, out_specs=P("rhs", "leaf"), check_vma=False
    )
```

profile of v0, /device:TPU:0, one launch (start us, length us, event | category | flops | bytes accessed | tf_op | source)
XLA Modules:
  0.0 303.4 jit_solution(3116804014196543378)
XLA Ops:
  7.4 2.7 slice.92
  19.9 2.8 copy.123
  39.2 2.9 collective-permute-start.12
  43.5 5.2 %collective-permute-start.10 = (bf16[32,2,64]{2,0,1:T(8,128)(2,1)}, bf16[32,2,64]{2,0,1:T(8,128)(2,1)}, u32[]{:S(2)}, u32[]{:S(2)}) collective-permute-start(bf16[32,2,64]{2,0,1:T(8,128)(2,1)} %bitcast_reduce_fusion.7), channel_id=1, source_target_pairs={{0,2},{2,4},{4,6},{6,8},{8,10},{10,12},{12,14},{14,16},{16,18},{18... | collective-permute-start | bytes 24584 | tf_op jit(solution)/shard_map/ppermute | solution.py:16
  49.9 4.3 %collective-permute-start.8 = (bf16[32,4,64]{2,0,1:T(8,128)(2,1)}, bf16[32,4,64]{2,0,1:T(8,128)(2,1)}, u32[]{:S(2)}, u32[]{:S(2)}) collective-permute-start(bf16[32,4,64]{2,0,1:T(8,128)(2,1)} %bitcast_reduce_fusion.5), channel_id=1, source_target_pairs={{0,2},{2,4},{4,6},{6,8},{8,10},{10,12},{12,14},{14,16},{16,18},{18... | collective-permute-start | bytes 49160 | tf_op jit(solution)/shard_map/ppermute | solution.py:16
  58.1 21.9 %all_gather.6 = f32[32,16,64]{2,0,1:T(8,128)S(1)} all-gather(f32[32,1,64]{2,0,1:T(8,128)S(1)} %convolution_bitcast_fusion.8), channel_id=1, replica_groups=mesh['leaf'=16,'rhs'=2] {'leaf'}, dimensions={1}, use_global_device_ids=true | all-gather | bytes 139264 | tf_op jit(solution)/shard_map/all_gather | solution.py:112
  87.1 11.2 %all_gather.7 = bf16[64,4096]{1,0:T(8,128)(2,1)} all-gather(bf16[32,4096]{1,0:T(8,128)(2,1)} %param.11), channel_id=1, replica_groups=mesh['leaf'=16,'rhs'=2] {'rhs'}, dimensions={0}, use_global_device_ids=true | all-gather | bytes 786432 | tf_op jit(solution)/shard_map/all_gather | solution.py:166
  108.9 5.8 %slice.105 = bf16[1,4,64,64]{0,3,2,1:T(8,128)(2,1)} slice(bf16[127,4,64,64]{0,3,2,1:T(8,128)(2,1)} %param.14), slice={[126:127], [0:4], [0:64], [0:64]} | slice | bytes 65536 | tf_op jit(solution)/shard_map/slice | solution.py:103
  114.7 3.2 %slice.102 = bf16[2,4,64,64]{0,3,2,1:T(8,128)(2,1)} slice(bf16[127,4,64,64]{0,3,2,1:T(8,128)(2,1)S(1)} %copy-done.1), slice={[124:126], [0:4], [0:64], [0:64]} | slice | bytes 131072 | tf_op jit(solution)/shard_map/slice | solution.py:103
  117.9 3.2 %slice.99 = bf16[4,4,64,64]{0,3,2,1:T(8,128)(2,1)} slice(bf16[127,4,64,64]{0,3,2,1:T(8,128)(2,1)S(1)} %copy-done.1), slice={[120:124], [0:4], [0:64], [0:64]} | slice | bytes 262144 | tf_op jit(solution)/shard_map/slice | solution.py:103
  121.1 3.2 %slice.96 = bf16[8,4,64,64]{0,3,2,1:T(8,128)(2,1)} slice(bf16[127,4,64,64]{0,3,2,1:T(8,128)(2,1)S(1)} %copy-done.1), slice={[112:120], [0:4], [0:64], [0:64]} | slice | bytes 524288 | tf_op jit(solution)/shard_map/slice | solution.py:103
  124.3 3.2 %slice.93 = bf16[16,4,64,64]{0,3,2,1:T(8,128)(2,1)} slice(bf16[127,4,64,64]{0,3,2,1:T(8,128)(2,1)S(1)} %copy-done.1), slice={[96:112], [0:4], [0:64], [0:64]} | slice | bytes 1048576 | tf_op jit(solution)/shard_map/slice | solution.py:103
  127.5 3.2 %slice.90 = bf16[32,4,64,64]{0,3,2,1:T(8,128)(2,1)} slice(bf16[127,4,64,64]{0,3,2,1:T(8,128)(2,1)S(1)} %copy-done.1), slice={[64:96], [0:4], [0:64], [0:64]} | slice | bytes 2097152 | tf_op jit(solution)/shard_map/slice | solution.py:103
  130.7 4.6 %copy.132 = bf16[1,4,64,64]{3,2,1,0:T(8,128)(2,1)} copy(bf16[1,4,64,64]{0,3,2,1:T(8,128)(2,1)} %slice.105) | data formatting | bytes 65536
  136.0 4.7 %copy.130 = bf16[2,4,64,64]{3,2,1,0:T(8,128)(2,1)} copy(bf16[2,4,64,64]{0,3,2,1:T(8,128)(2,1)} %slice.102) | data formatting | bytes 131072
  141.4 4.9 %copy.128 = bf16[4,4,64,64]{3,2,1,0:T(8,128)(2,1)} copy(bf16[4,4,64,64]{0,3,2,1:T(8,128)(2,1)} %slice.99) | data formatting | bytes 262144
  146.8 3.7 %copy.126 = bf16[8,4,64,64]{3,2,1,0:T(8,128)(2,1)S(1)} copy(bf16[8,4,64,64]{0,3,2,1:T(8,128)(2,1)} %slice.96) | data formatting | bytes 524288
  151.2 5.0 %copy.124 = bf16[16,4,64,64]{3,2,1,0:T(8,128)(2,1)} copy(bf16[16,4,64,64]{0,3,2,1:T(8,128)(2,1)} %slice.93) | data formatting | bytes 1048576
  156.9 6.1 %copy.122 = bf16[32,4,64,64]{3,2,1,0:T(8,128)(2,1)} copy(bf16[32,4,64,64]{0,3,2,1:T(8,128)(2,1)} %slice.90) | data formatting | bytes 2097152
  164.3 7.3 %copy.120 = bf16[64,4,64,64]{3,2,1,0:T(8,128)(2,1)} copy(bf16[64,4,64,64]{0,3,2,1:T(8,128)(2,1)} %bitcast.214) | data formatting | bytes 4194304
  173.1 3.7 %collective-permute-start.6 = (bf16[32,8,64]{2,0,1:T(8,128)(2,1)}, bf16[32,8,64]{2,0,1:T(8,128)(2,1)}, u32[]{:S(2)}, u32[]{:S(2)}) collective-permute-start(bf16[32,8,64]{2,0,1:T(8,128)(2,1)} %copy-done.12), channel_id=1, source_target_pairs={{0,2},{2,4},{4,6},{6,8},{8,10},{10,12},{12,14},{14,16},{16,18},{18... | collective-permute-start | bytes 98312 | tf_op jit(solution)/shard_map/ppermute | solution.py:16
  183.1 3.7 %collective-permute-start.4 = (bf16[32,16,64]{2,0,1:T(8,128)(2,1)}, bf16[32,16,64]{2,0,1:T(8,128)(2,1)}, u32[]{:S(2)}, u32[]{:S(2)}) collective-permute-start(bf16[32,16,64]{2,0,1:T(8,128)(2,1)} %copy-done.9), channel_id=1, source_target_pairs={{0,2},{2,4},{4,6},{6,8},{8,10},{10,12},{12,14},{14,16},{16,18},{18... | collective-permute-start | bytes 196616 | tf_op jit(solution)/shard_map/ppermute | solution.py:16
  193.4 4.4 %collective-permute-start.2 = (bf16[32,32,64]{2,0,1:T(8,128)(2,1)}, bf16[32,32,64]{2,0,1:T(8,128)(2,1)}, u32[]{:S(2)}, u32[]{:S(2)}) collective-permute-start(bf16[32,32,64]{2,0,1:T(8,128)(2,1)} %bitcast_reduce_fusion), channel_id=1, source_target_pairs={{0,2},{2,4},{4,6},{6,8},{8,10},{10,12},{12,14},{14,16},{16,18},{18... | collective-permute-start | bytes 393224 | tf_op jit(solution)/shard_map/ppermute | solution.py:16
  203.5 3.7 %collective-permute-start.14 = (bf16[64,4096]{1,0:T(8,128)(2,1)}, bf16[64,4096]{1,0:T(8,128)(2,1)}, u32[]{:S(2)}, u32[]{:S(2)}) collective-permute-start(bf16[64,4096]{1,0:T(8,128)(2,1)} %all_gather.7), channel_id=1, source_target_pairs={{0,2},{2,4},{4,6},{6,8},{8,10},{10,12},{12,14},{14,16},{16,18},{18... | collective-permute-start | bytes 1572872 | tf_op jit(solution)/shard_map/ppermute | solution.py:16
  220.8 4.5 %collective-permute-start = (bf16[32,64,64]{2,0,1:T(8,128)(2,1)S(1)}, bf16[32,64,64]{2,0,1:T(8,128)(2,1)}, u32[]{:S(2)}, u32[]{:S(2)}) collective-permute-start(bf16[32,64,64]{2,0,1:T(8,128)(2,1)S(1)} %copy-done.6), channel_id=1, source_target_pairs={{0,2},{2,4},{4,6},{6,8},{8,10},{10,12},{12,14},{14,16},{16,18},{18... | collective-permute-start | bytes 786440 | tf_op jit(solution)/shard_map/ppermute | solution.py:16
  234.3 5.5 %reshape.437 = bf16[64,192,64]{2,1,0:T(8,128)(2,1)} reshape(bf16[64,12288]{1,0:T(8,128)(2,1)} %pad_maximum_fusion.1) | data formatting | bytes 3145728 | tf_op jit(solution)/shard_map/reshape | solution.py:168
  239.8 5.6 %copy.111 = bf16[64,192,64]{2,0,1:T(8,128)(2,1)} copy(bf16[64,192,64]{2,1,0:T(8,128)(2,1)} %reshape.437) | data formatting | bytes 3145728 | tf_op jit(solution)/shard_map/reshape | solution.py:168
  245.5 5.1 %gather_fusion.8 = bf16[256,64,64]{2,1,0:T(8,128)(2,1)} fusion(bf16[64,192,64]{2,0,1:T(8,128)(2,1)} %copy.111, s32[1024]{0:T(1024)} %pad_clamp_fusion), kind=kCustom, calls=%fused_computation.8 | custom fusion | bytes 4195328 | tf_op jit(solution)/shard_map/jit(_take)/gather | solution.py:170
  250.6 6.2 %fusion.7 = f32[64,64,64]{2,0,1:T(8,128)} fusion(bf16[64,4,64,64]{3,2,1,0:T(8,128)(2,1)} %param.20, bf16[64,64,4,64]{3,0,2,1:T(8,128)(2,1)} %bitcast.218, pred[64,4]{1,0:T(8,128)(4,1)S(1)} %copy-done.17), kind=kOutput, calls=%fused_computation.16 | convolution fusion | flops 135266304 | bytes 5243136 | tf_op jit(solution)/shard_map/rijq,ijpq->rip/dot_general | solution.py:174
  265.8 2.9 gather_fusion.1
  277.0 12.5 %reduce-scatter.2.cloned.1.call-done = f32[32,64,64]{2,0,1:T(8,128)} async-done(((f32[64,64,64]{2,0,1:T(8,128)}), f32[32,64,64]{2,0,1:T(8,128)}) %reduce-scatter.2.cloned.1.call-update) | async-done | bytes 524304 | tf_op jit(solution)/shard_map/reduce_scatter | solution.py:173
  289.5 5.1 %fusion.20 = bf16[32,64,64]{2,0,1:T(8,128)(2,1)S(1)} fusion(f32[32,64,64]{2,0,1:T(8,128)} %reduce-scatter.2.cloned.1.call-done, bf16[64,64,64]{2,1,0:T(8,128)(2,1)S(1)} %copy-done, f32[64,32,64]{2,1,0:T(8,128)} %fusion.103, bf16[64,4,64,64]{3,2,1,0:T(8,128)(2,1)} %copy.120, bf16[32,64,4,64]{3,0,2,1:T(8,128)(2,1)} %bitcast.216, pred[64,4]{1,0:T(8,128)(4,1)S(1)} %copy-done.15), kind=kOutput, calls=%fused_computation.24 | convolution fusion | flops 84934656 | bytes 4980992 | tf_op jit(solution)/shard_map/rik,ipk->rip/dot_general | solution.py:165
  (192 shorter events, 116.1 us)
Async XLA Ops:
  7.4 23.4 %copy-start = (bf16[64,64,64]{2,1,0:T(8,128)(2,1)S(1)}, bf16[64,64,64]{2,1,0:T(8,128)(2,1)}, u32[]{:S(2)}) copy-start(bf16[64,64,64]{2,1,0:T(8,128)(2,1)} %param.12) | copy-start | bytes 1572868
  7.4 5.3 %copy-start.2 = (bf16[127,64,64]{0,2,1:T(8,128)(2,1)S(1)}, bf16[127,64,64]{0,2,1:T(8,128)(2,1)}, u32[]{:S(2)}) copy-start(bf16[127,64,64]{0,2,1:T(8,128)(2,1)} %param.13) | copy-start | bytes 3121156
  7.4 207.1 %all-reduce.2.cloned.1.call-start = ((), (), s32[]{:S(2)}) async-start(), calls=%async_computation.1 | async-start | bytes 524288 | tf_op jit(solution)/shard_map/psum | solution.py:144
  30.8 5.4 %copy-start.11 = (bf16[4,64,64]{2,1,0:T(8,128)(2,1)S(1)}, bf16[4,64,64]{2,1,0:T(8,128)(2,1)}, u32[]{:S(2)}) copy-start(bf16[4,64,64]{2,1,0:T(8,128)(2,1)} %copy.129) | copy-start | bytes 98308
  30.8 6.9 %copy-start.13 = (bf16[2,64,64]{2,1,0:T(8,128)(2,1)S(1)}, bf16[2,64,64]{2,1,0:T(8,128)(2,1)}, u32[]{:S(2)}) copy-start(bf16[2,64,64]{2,1,0:T(8,128)(2,1)} %copy.131) | copy-start | bytes 49156
  32.5 23.1 %copy-start.19 = (s32[4]{0:T(128)S(1)}, s32[4]{0:T(128)}, u32[]{:S(2)}) copy-start(s32[4]{0:T(128)} %param.19) | copy-start | bytes 52
  39.2 132.4 %collective-permute-start.12 = (bf16[32,1,64]{2,0,1:T(8,128)(2,1)}, bf16[32,1,64]{2,0,1:T(8,128)(2,1)}, u32[]{:S(2)}, u32[]{:S(2)}) collective-permute-start(bf16[32,1,64]{2,0,1:T(8,128)(2,1)} %bitcast.42), channel_id=1, source_target_pairs={{0,2},{2,4},{4,6},{6,8},{8,10},{10,12},{12,14},{14,16},{16,18},{18... | collective-permute-start | bytes 12296 | tf_op jit(solution)/shard_map/ppermute | solution.py:16
  42.2 130.9 %collective-permute-start.13 = (bf16[32,1,64]{2,0,1:T(8,128)(2,1)}, bf16[32,1,64]{2,0,1:T(8,128)(2,1)}, u32[]{:S(2)}, u32[]{:S(2)}) collective-permute-start(bf16[32,1,64]{2,0,1:T(8,128)(2,1)} %bitcast.42), channel_id=1, source_target_pairs={{2,0},{4,2},{6,4},{8,6},{10,8},{12,10},{14,12},{16,14},{18,16},{20... | collective-permute-start | bytes 12296 | tf_op jit(solution)/shard_map/ppermute | solution.py:17
  43.5 138.4 %collective-permute-start.10 = (bf16[32,2,64]{2,0,1:T(8,128)(2,1)}, bf16[32,2,64]{2,0,1:T(8,128)(2,1)}, u32[]{:S(2)}, u32[]{:S(2)}) collective-permute-start(bf16[32,2,64]{2,0,1:T(8,128)(2,1)} %bitcast_reduce_fusion.7), channel_id=1, source_target_pairs={{0,2},{2,4},{4,6},{6,8},{8,10},{10,12},{12,14},{14,16},{16,18},{18... | collective-permute-start | bytes 24584 | tf_op jit(solution)/shard_map/ppermute | solution.py:16
  48.6 134.5 %collective-permute-start.11 = (bf16[32,2,64]{2,0,1:T(8,128)(2,1)}, bf16[32,2,64]{2,0,1:T(8,128)(2,1)}, u32[]{:S(2)}, u32[]{:S(2)}) collective-permute-start(bf16[32,2,64]{2,0,1:T(8,128)(2,1)} %bitcast_reduce_fusion.7), channel_id=1, source_target_pairs={{2,0},{4,2},{6,4},{8,6},{10,8},{12,10},{14,12},{16,14},{18,16},{20... | collective-permute-start | bytes 24584 | tf_op jit(solution)/shard_map/ppermute | solution.py:17
  49.9 142.2 %collective-permute-start.8 = (bf16[32,4,64]{2,0,1:T(8,128)(2,1)}, bf16[32,4,64]{2,0,1:T(8,128)(2,1)}, u32[]{:S(2)}, u32[]{:S(2)}) collective-permute-start(bf16[32,4,64]{2,0,1:T(8,128)(2,1)} %bitcast_reduce_fusion.5), channel_id=1, source_target_pairs={{0,2},{2,4},{4,6},{6,8},{8,10},{10,12},{12,14},{14,16},{16,18},{18... | collective-permute-start | bytes 49160 | tf_op jit(solution)/shard_map/ppermute | solution.py:16
  85.6 203.9 %reduce-scatter.2.cloned.1.call-start = ((), (), s32[]{:S(2)}) async-start(), calls=%async_computation.2 | async-start | bytes 3145728 | tf_op jit(solution)/shard_map/reduce_scatter | solution.py:173
  108.9 5.8 %copy-start.1 = (bf16[127,4,64,64]{0,3,2,1:T(8,128)(2,1)S(1)}, bf16[127,4,64,64]{0,3,2,1:T(8,128)(2,1)}, u32[]{:S(2)}) copy-start(bf16[127,4,64,64]{0,3,2,1:T(8,128)(2,1)} %param.14) | copy-start | bytes 12484612
  171.6 49.1 %copy-start.6 = (bf16[32,64,64]{2,0,1:T(8,128)(2,1)S(1)}, bf16[32,64,64]{2,0,1:T(8,128)(2,1)}, u32[]{:S(2)}) copy-start(bf16[32,64,64]{2,0,1:T(8,128)(2,1)} %copy-done.5) | copy-start | bytes 786436
  171.7 21.8 %collective-permute-start.9 = (bf16[32,4,64]{2,0,1:T(8,128)(2,1)}, bf16[32,4,64]{2,0,1:T(8,128)(2,1)}, u32[]{:S(2)}, u32[]{:S(2)}) collective-permute-start(bf16[32,4,64]{2,0,1:T(8,128)(2,1)} %bitcast_reduce_fusion.5), channel_id=1, source_target_pairs={{2,0},{4,2},{6,4},{8,6},{10,8},{12,10},{14,12},{16,14},{18,16},{20... | collective-permute-start | bytes 49160 | tf_op jit(solution)/shard_map/ppermute | solution.py:17
  173.1 30.4 %collective-permute-start.6 = (bf16[32,8,64]{2,0,1:T(8,128)(2,1)}, bf16[32,8,64]{2,0,1:T(8,128)(2,1)}, u32[]{:S(2)}, u32[]{:S(2)}) collective-permute-start(bf16[32,8,64]{2,0,1:T(8,128)(2,1)} %copy-done.12), channel_id=1, source_target_pairs={{0,2},{2,4},{4,6},{6,8},{8,10},{10,12},{12,14},{14,16},{16,18},{18... | collective-permute-start | bytes 98312 | tf_op jit(solution)/shard_map/ppermute | solution.py:16
  181.8 25.4 %collective-permute-start.7 = (bf16[32,8,64]{2,0,1:T(8,128)(2,1)}, bf16[32,8,64]{2,0,1:T(8,128)(2,1)}, u32[]{:S(2)}, u32[]{:S(2)}) collective-permute-start(bf16[32,8,64]{2,0,1:T(8,128)(2,1)} %copy-done.12), channel_id=1, source_target_pairs={{2,0},{4,2},{6,4},{8,6},{10,8},{12,10},{14,12},{16,14},{18,16},{20... | collective-permute-start | bytes 98312 | tf_op jit(solution)/shard_map/ppermute | solution.py:17
  183.1 36.3 %collective-permute-start.4 = (bf16[32,16,64]{2,0,1:T(8,128)(2,1)}, bf16[32,16,64]{2,0,1:T(8,128)(2,1)}, u32[]{:S(2)}, u32[]{:S(2)}) collective-permute-start(bf16[32,16,64]{2,0,1:T(8,128)(2,1)} %copy-done.9), channel_id=1, source_target_pairs={{0,2},{2,4},{4,6},{6,8},{8,10},{10,12},{12,14},{14,16},{16,18},{18... | collective-permute-start | bytes 196616 | tf_op jit(solution)/shard_map/ppermute | solution.py:16
  192.1 28.6 %collective-permute-start.5 = (bf16[32,16,64]{2,0,1:T(8,128)(2,1)}, bf16[32,16,64]{2,0,1:T(8,128)(2,1)}, u32[]{:S(2)}, u32[]{:S(2)}) collective-permute-start(bf16[32,16,64]{2,0,1:T(8,128)(2,1)} %copy-done.9), channel_id=1, source_target_pairs={{2,0},{4,2},{6,4},{8,6},{10,8},{12,10},{14,12},{16,14},{18,16},{20... | collective-permute-start | bytes 196616 | tf_op jit(solution)/shard_map/ppermute | solution.py:17
  193.4 69.9 %collective-permute-start.2 = (bf16[32,32,64]{2,0,1:T(8,128)(2,1)}, bf16[32,32,64]{2,0,1:T(8,128)(2,1)}, u32[]{:S(2)}, u32[]{:S(2)}) collective-permute-start(bf16[32,32,64]{2,0,1:T(8,128)(2,1)} %bitcast_reduce_fusion), channel_id=1, source_target_pairs={{0,2},{2,4},{4,6},{6,8},{8,10},{10,12},{12,14},{14,16},{16,18},{18... | collective-permute-start | bytes 393224 | tf_op jit(solution)/shard_map/ppermute | solution.py:16
  203.5 26.9 %collective-permute-start.14 = (bf16[64,4096]{1,0:T(8,128)(2,1)}, bf16[64,4096]{1,0:T(8,128)(2,1)}, u32[]{:S(2)}, u32[]{:S(2)}) collective-permute-start(bf16[64,4096]{1,0:T(8,128)(2,1)} %all_gather.7), channel_id=1, source_target_pairs={{0,2},{2,4},{4,6},{6,8},{8,10},{10,12},{12,14},{14,16},{16,18},{18... | collective-permute-start | bytes 1572872 | tf_op jit(solution)/shard_map/ppermute | solution.py:16
  207.2 24.4 %collective-permute-start.15 = (bf16[64,4096]{1,0:T(8,128)(2,1)}, bf16[64,4096]{1,0:T(8,128)(2,1)}, u32[]{:S(2)}, u32[]{:S(2)}) collective-permute-start(bf16[64,4096]{1,0:T(8,128)(2,1)} %all_gather.7), channel_id=1, source_target_pairs={{2,0},{4,2},{6,4},{8,6},{10,8},{12,10},{14,12},{16,14},{18,16},{20... | collective-permute-start | bytes 1572872 | tf_op jit(solution)/shard_map/ppermute | solution.py:17
  214.4 13.5 %slice-start = ((f32[32,16,64]{2,1,0:T(8,128)}), f32[32,8,64]{2,1,0:T(8,128)S(1)}, s32[]{:S(2)}) async-start(f32[32,16,64]{2,1,0:T(8,128)} %all-reduce.2.cloned.1.call-done), calls=%async_computation.3 | async-start | bytes 262144 | tf_op jit(solution)/shard_map/slice | solution.py:39
  219.4 43.9 %collective-permute-start.3 = (bf16[32,32,64]{2,0,1:T(8,128)(2,1)}, bf16[32,32,64]{2,0,1:T(8,128)(2,1)}, u32[]{:S(2)}, u32[]{:S(2)}) collective-permute-start(bf16[32,32,64]{2,0,1:T(8,128)(2,1)} %bitcast_reduce_fusion), channel_id=1, source_target_pairs={{2,0},{4,2},{6,4},{8,6},{10,8},{12,10},{14,12},{16,14},{18,16},{20... | collective-permute-start | bytes 393224 | tf_op jit(solution)/shard_map/ppermute | solution.py:17
  220.8 52.4 %collective-permute-start = (bf16[32,64,64]{2,0,1:T(8,128)(2,1)S(1)}, bf16[32,64,64]{2,0,1:T(8,128)(2,1)}, u32[]{:S(2)}, u32[]{:S(2)}) collective-permute-start(bf16[32,64,64]{2,0,1:T(8,128)(2,1)S(1)} %copy-done.6), channel_id=1, source_target_pairs={{0,2},{2,4},{4,6},{6,8},{8,10},{10,12},{12,14},{14,16},{16,18},{18... | collective-permute-start | bytes 786440 | tf_op jit(solution)/shard_map/ppermute | solution.py:16
  230.3 42.8 %collective-permute-start.1 = (bf16[32,64,64]{2,0,1:T(8,128)(2,1)S(1)}, bf16[32,64,64]{2,0,1:T(8,128)(2,1)}, u32[]{:S(2)}, u32[]{:S(2)}) collective-permute-start(bf16[32,64,64]{2,0,1:T(8,128)(2,1)S(1)} %copy-done.6), channel_id=1, source_target_pairs={{2,0},{4,2},{6,4},{8,6},{10,8},{12,10},{14,12},{16,14},{18,16},{20... | collective-permute-start | bytes 786440 | tf_op jit(solution)/shard_map/ppermute | solution.py:17
  245.5 5.1 %copy-start.17 = (pred[64,4]{1,0:T(8,128)(4,1)S(1)}, pred[64,4]{1,0:T(8,128)(4,1)}, u32[]{:S(2)}) copy-start(pred[64,4]{1,0:T(8,128)(4,1)} %copy.109) | copy-start | bytes 772
  250.6 6.2 %copy-start.18 = (pred[16,4]{1,0:T(8,128)(4,1)S(1)}, pred[16,4]{1,0:T(8,128)(4,1)}, u32[]{:S(2)}) copy-start(pred[16,4]{1,0:T(8,128)(4,1)} %copy.85) | copy-start | bytes 196
  256.8 5.3 %copy-start.4 = (bf16[32,64,64]{2,1,0:T(8,128)(2,1)S(1)}, bf16[32,64,64]{2,1,0:T(8,128)(2,1)}, u32[]{:S(2)}) copy-start(bf16[32,64,64]{2,1,0:T(8,128)(2,1)} %copy.123) | copy-start | bytes 786436
  261.8 7.0 %copy-start.16 = (pred[32,4]{1,0:T(8,128)(4,1)S(1)}, pred[32,4]{1,0:T(8,128)(4,1)}, u32[]{:S(2)}) copy-start(pred[32,4]{1,0:T(8,128)(4,1)} %copy.81) | copy-start | bytes 388
  263.3 5.4 %copy-start.8 = (f32[32,32,64]{2,1,0:T(8,128)S(1)}, f32[32,32,64]{2,1,0:T(8,128)}, u32[]{:S(2)}) copy-start(f32[32,32,64]{2,1,0:T(8,128)} %fusion.102) | copy-start | bytes 786436
  273.1 16.4 %copy-start.15 = (pred[64,4]{1,0:T(8,128)(4,1)S(1)}, pred[64,4]{1,0:T(8,128)(4,1)}, u32[]{:S(2)}) copy-start(pred[64,4]{1,0:T(8,128)(4,1)} %copy.77) | copy-start | bytes 772
  (7 other events, 18.6 us)
Sparse Core Ops, SparseCore 0:
  85.7 86.1 all-reduce.1
Sparse Core Ops, SparseCore 1:
  256.9 32.6 reduce-scatter.1
where the time goes:
time: 307 us; the launch traced here: 303 us
  local copies, waits for them, and re-layouts  127 us (41%)
  matrix products  46.7 us (15%)
  starting transfers between devices  42.8 us (14%)
  blocking collectives  33 us (11%)
  other arithmetic  26.4 us (9%)
  between operations  15.4 us (5%)
  waiting for transfers between devices  12.5 us (4%)
    unnamed x54, local copies, waits for them, and re-layouts  51 us
    ppermute x8, starting transfers between devices, padded(): before = lax.ppermute(last, axis, up)  32.4 us
    all_gather x1, blocking collectives, shards(): root_terms = lax.all_gather(root_term, 'leaf', axis=1, tiled=True)  21.9 us
    slice x6, local copies, waits for them, and re-layouts, shards(): coupling[couple_first_node:couple_first_node + couple_node_count]  21.8 us
    gather x7, local copies, waits for them, and re-layouts, shards(): jnp.take(extended, source_ids.reshape(-1), axis=1)  15.5 us
    concatenate x8, other arithmetic, padded(): array = jnp.concatenate([before, array, after], axis=dim)  13.6 us
    reduce_scatter x1, waiting for transfers between devices, shards(): lax.psum_scatter(jnp.einsum('rijq,ijpq->rip', gathered, near_blocks, pref...  12.5 us
    dot_general x6, matrix products, shards(): jnp.einsum('rtkm,tkmn->rtn', picked, coupling[couple_first_node:couple_fi...  12 us
  transfers between devices with their start and end apart: 18, of which 1 were waited for; matrix products, arithmetic and copies ran while one was open for 53% of the time, Pallas kernels for 0%

commit v1 on v0

v1 whole, which is shorter than its diff:
```python
import functools

import jax
import jax.numpy as jnp
from jax import lax
from jax.experimental import pallas as pl
from jax.experimental.pallas import tpu as pltpu
from jax.sharding import PartitionSpec as P

MESH = pl.DeviceIdType.MESH
NT = (((1,), (1,)), ((), ()))
NN = (((1,), (0,)), ((), ()))
f32 = jnp.float32
bf16 = jnp.bfloat16


def mm(a, b, dims=NN):
    return lax.dot_general(a, b, dims, preferred_element_type=f32)


def mm_split(a, b, dims):
    high = a.astype(bf16)
    low = (a - high.astype(f32)).astype(bf16)
    return mm(high, b, dims) + mm(low, b, dims)


def level_table(leaf_count):
    layout = []
    first, count, pair = 0, leaf_count, 0
    while count >= 1:
        layout.append((first, count, pair))
        first += count
        pair += max(count // 2, 1)
        count //= 2
    return layout


def loop(count, body, unroll):
    unroll = min(unroll, count)
    while count % unroll:
        unroll -= 1

    def step(i, carry):
        for u in range(unroll):
            body(i * unroll + u)
        return carry

    if count == unroll:
        step(0, 0)
    else:
        lax.fori_loop(0, count // unroll, step, 0)


def kernel(
    roots_n,
    vec, basis_h, trans_h, coup_h, near_h,
    cs, ns, tt, ts, top_t, top_c,
    out,
    vbuf, pts, basis, trans, coup, near,
    cp, halo, cl, field, down, near_own, near_send, near_recv,
    roots, uc, g, top_recv,
    local_sem, vs_sem, vr_sem, hs_sem, hr_sem, ns_sem, nr_sem, rs_sem, rr_sem, ts_sem, tr_sem,
):
    n = roots_n
    leaves = basis.shape[0]
    width = basis.shape[1]
    rows = vec.shape[0]
    layout = level_table(leaves)
    pairs = leaves // 2
    slots = coup.shape[1]
    near_slots = near.shape[1]
    top_blocks = top_c.shape[0]
    me = lax.axis_index("leaf")
    mine = lax.axis_index("rhs")
    other = 1 - mine
    has_left, has_right = me > 0, me < n - 1

    def peer_of(i):
        return lax.rem(me + i, n)

    barrier = pltpu.get_barrier_semaphore()

    def greet(i, carry):
        pl.semaphore_signal(barrier, inc=1, device_id=(peer_of(i), mine), device_id_type=MESH)
        return carry

    lax.fori_loop(1, n, greet, 0)
    pl.semaphore_signal(barrier, inc=1, device_id=(me, other), device_id_type=MESH)

    @pl.when(has_left)
    def _():
        pl.semaphore_signal(barrier, inc=1, device_id=(me - 1, other), device_id_type=MESH)

    @pl.when(has_right)
    def _():
        pl.semaphore_signal(barrier, inc=1, device_id=(me + 1, other), device_id_type=MESH)

    local = [
        pltpu.make_async_copy(src, dst, local_sem.at[i])
        for i, (src, dst) in enumerate(
            ((vec, vbuf.at[1, 0]), (basis_h, basis), (trans_h, trans), (near_h, near), (coup_h, coup))
        )
    ]
    for copy in local:
        copy.start()

    pl.semaphore_wait(barrier, n + jnp.where(has_left, 1, 0) + jnp.where(has_right, 1, 0))

    def vec_send(place, half):
        target = (me + (1 - place), mine if half == 0 else other)
        return pltpu.make_async_remote_copy(
            src_ref=vec, dst_ref=vbuf.at[place, half],
            send_sem=vs_sem.at[place, half], recv_sem=vr_sem.at[place, half],
            device_id=target, device_id_type=MESH,
        )

    def halo_send(place, part):
        part_pairs = pl.ds(0, pairs) if part == 0 else pl.ds(pairs, cp.shape[0] - pairs)
        return pltpu.make_async_remote_copy(
            src_ref=cp.at[part_pairs], dst_ref=halo.at[place, part_pairs],
            send_sem=hs_sem.at[place, part], recv_sem=hr_sem.at[place, part],
            device_id=(me + (1 - 2 * place), mine), device_id_type=MESH,
        )

    sends_right, sends_left = has_right, has_left
    vec_send(1, 1).start()

    @pl.when(sends_right)
    def _():
        vec_send(0, 0).start()
        vec_send(0, 1).start()

    @pl.when(sends_left)
    def _():
        vec_send(2, 0).start()
        vec_send(2, 1).start()

    local[0].wait()
    local[1].wait()

    def store_pair(pair_index, node_index, a, b):
        cp[pair_index] = jnp.concatenate([a, b], axis=1)
        cl[node_index] = a
        cl[node_index + 1] = b

    def leaf_up(p):
        x = vbuf[1, 0, :, pl.ds(pl.multiple_of(p * 2 * width, 2 * width), 2 * width)]
        x0, x1 = x[:, :width], x[:, width:]
        c0 = mm(x0, basis[2 * p]).astype(bf16)
        c1 = mm(x1, basis[2 * p + 1]).astype(bf16)
        store_pair(p, leaves + 2 * p, c0, c1)

    loop(pairs, leaf_up, 4)

    @pl.when(sends_right)
    def _():
        halo_send(0, 0).start()

    @pl.when(sends_left)
    def _():
        halo_send(1, 0).start()

    local[2].wait()
    for height in range(1, len(layout)):
        below_first, below_count, below_pair = layout[height - 1]
        first, count, pair = layout[height]

        def lift(q):
            w = trans[pl.ds(below_first + 2 * q, 2)].reshape(2 * width, width)
            return mm(cp[below_pair + q], w).astype(bf16)

        if count > 1:
            def up(p):
                store_pair(pair + p, 3 * first + count + 2 * p, lift(2 * p), lift(2 * p + 1))

            loop(count // 2, up, 4)
        else:
            c = lift(0)
            cp[pair] = jnp.concatenate([c, c], axis=1)
            cl[3 * first + count] = c
    root_row = layout[-1][0]
    root_pair = layout[-1][2]
    root_term = mm(cp[root_pair][:, :width], trans[root_row])
    roots[me] = root_term

    def root_copy(i):
        return pltpu.make_async_remote_copy(
            src_ref=roots.at[me], dst_ref=roots.at[me],
            send_sem=rs_sem.at[i], recv_sem=rr_sem.at[me],
            device_id=(peer_of(i), mine), device_id_type=MESH,
        )

    def root_recv(i):
        source = peer_of(i)
        return pltpu.make_async_remote_copy(
            src_ref=roots.at[source], dst_ref=roots.at[source],
            send_sem=rs_sem.at[i], recv_sem=rr_sem.at[source],
            device_id=(source, mine), device_id_type=MESH,
        )

    def send_roots(i, carry):
        root_copy(i).start()
        return carry

    lax.fori_loop(1, n, send_roots, 0)

    @pl.when(sends_right)
    def _():
        halo_send(0, 1).start()

    @pl.when(sends_left)
    def _():
        halo_send(1, 1).start()

    def unpack_points(place, half):
        def body(p):
            x = vbuf[place, half, :, pl.ds(pl.multiple_of(p * 2 * width, 2 * width), 2 * width)]
            pts[place * leaves + 2 * p, half * rows:(half + 1) * rows, :] = x[:, :width]
            pts[place * leaves + 2 * p + 1, half * rows:(half + 1) * rows, :] = x[:, width:]

        loop(pairs, body, 8)

    unpack_points(1, 0)

    @pl.when(jnp.logical_not(has_left))
    def _():
        vbuf[0] = jnp.zeros(vbuf.shape[1:], bf16)
        halo[0] = jnp.zeros(halo.shape[1:], bf16)

    @pl.when(jnp.logical_not(has_right))
    def _():
        vbuf[2] = jnp.zeros(vbuf.shape[1:], bf16)
        halo[1] = jnp.zeros(halo.shape[1:], bf16)

    vec_send(1, 1).wait_recv()
    unpack_points(1, 1)
    for half in range(2):
        @pl.when(has_left)
        def _():
            vec_send(0, half).wait_recv()

        unpack_points(0, half)

        @pl.when(has_right)
        def _():
            vec_send(2, half).wait_recv()

        unpack_points(2, half)

    local[3].wait()
    leaf_base = (me - 1) * leaves

    def near_leaf(i):
        total = None
        for j in range(near_slots):
            term = mm(pts[jnp.clip(ns[j, i] - leaf_base, 0, 3 * leaves - 1)], near[i, j], NT)
            total = term if total is None else total + term
        return total

    def near_pair(p):
        both = jnp.concatenate([near_leaf(2 * p), near_leaf(2 * p + 1)], axis=1)
        near_own[p] = both[:rows]
        near_send[p] = both[rows:].astype(bf16)

    chunks = near_recv_chunks = ns_sem.shape[0]
    chunk = pairs // chunks

    def near_copy(c):
        part = pl.ds(c * chunk, chunk)
        return pltpu.make_async_remote_copy(
            src_ref=near_send.at[part], dst_ref=near_recv.at[part],
            send_sem=ns_sem.at[c], recv_sem=nr_sem.at[c],
            device_id=(me, other), device_id_type=MESH,
        )

    for c in range(chunks):
        loop(chunk, lambda p: near_pair(c * chunk + p), 2)
        near_copy(c).start()

    def recv_roots(i, carry):
        root_recv(i).wait_recv()
        return carry

    lax.fori_loop(1, n, recv_roots, 0)
    half_n = n // 2
    uc[0] = jnp.zeros(uc.shape[1:], bf16)
    uc[1] = jnp.zeros(uc.shape[1:], bf16)
    loop(half_n, lambda j: uc.__setitem__(half_n + j, (roots[2 * j] + roots[2 * j + 1]).astype(bf16)), 4)
    size = half_n // 2
    while size >= 2:
        def upper_up(j):
            h = size + j
            x = mm(uc[2 * h], top_t[2 * h - 2]) + mm(uc[2 * h + 1], top_t[2 * h - 1])
            uc[h] = x.astype(bf16)

        loop(size, upper_up, 4)
        size //= 2
    terms = [mm(uc[ts[b]], top_c[b]) for b in range(top_blocks)]

    def upper_gather(j):
        h = j + 2
        total = None
        for b in range(top_blocks):
            term = terms[b] * (tt[b] == h).astype(f32)
            total = term if total is None else total + term
        g[h] = total

    loop(n - 2, upper_gather, 2)
    size = 2
    while size < half_n:
        def upper_down(j):
            h = size + j
            w = top_t[pl.ds(2 * h - 2, 2)].reshape(2 * width, width)
            x = mm_split(g[h], w, NT)
            g[2 * h] = g[2 * h] + x[:, :width]
            g[2 * h + 1] = g[2 * h + 1] + x[:, width:]

        loop(size, upper_down, 4)
        size *= 2

    def top_copy(i):
        peer = peer_of(i)
        return pltpu.make_async_remote_copy(
            src_ref=g.at[half_n + peer // 2], dst_ref=top_recv.at[me],
            send_sem=ts_sem.at[i], recv_sem=tr_sem.at[me],
            device_id=(peer, mine), device_id_type=MESH,
        )

    def top_wait(i):
        source = peer_of(i)
        return pltpu.make_async_remote_copy(
            src_ref=g.at[half_n + source // 2], dst_ref=top_recv.at[source],
            send_sem=ts_sem.at[i], recv_sem=tr_sem.at[source],
            device_id=(source, mine), device_id_type=MESH,
        )

    def send_top(i, carry):
        top_copy(i).start()
        return carry

    lax.fori_loop(1, n, send_top, 0)

    for part in range(2):
        @pl.when(has_left)
        def _():
            halo_send(0, part).wait_recv()

        @pl.when(has_right)
        def _():
            halo_send(1, part).wait_recv()

    for first, count, pair in layout:
        for place in range(2):
            base = 3 * first + 2 * place * count
            if count > 1:
                def unpack(p):
                    x = halo[place, pair + p]
                    cl[base + 2 * p] = x[:, :width]
                    cl[base + 2 * p + 1] = x[:, width:]

                loop(count // 2, unpack, 8)
            else:
                cl[base] = halo[place, pair][:, :width]

    local[4].wait()
    for first, count, pair in layout:
        base = 3 * first - (me - 1) * count

        def node_field(t):
            sources = [jnp.clip(base + cs[k, first + t], 0, cl.shape[0] - 1) for k in range(slots)]
            x = jnp.concatenate([cl[source] for source in sources], axis=1)
            return mm(x, coup[first + t].reshape(slots * width, width))

        if count > 1:
            def pair_field(p):
                field[pair + p] = jnp.concatenate([node_field(2 * p), node_field(2 * p + 1)], axis=1)

            loop(count // 2, pair_field, 4)
        else:
            root_field = node_field(0)

    def recv_top(i, total):
        top_wait(i).wait_recv()
        return total + top_recv[peer_of(i)]

    parent = lax.fori_loop(1, n, recv_top, g[half_n + me // 2])
    root_down = (root_field + mm_split(parent, trans[root_row], NT)).astype(bf16)

    def step_down(height, q, x):
        first, count, pair = layout[height]
        w = trans[pl.ds(first + 2 * q, 2)].reshape(2 * width, width)
        return (field[pair + q] + mm(x, w, NT)).astype(bf16)

    top_height = len(layout) - 2
    down[layout[top_height][2]] = step_down(top_height, 0, root_down)
    for height in range(top_height - 1, 0, -1):
        pair = layout[height][2]
        above = layout[height + 1][2]

        def descend(p):
            x = down[above + p]
            down[pair + 2 * p] = step_down(height, 2 * p, x[:, :width])
            down[pair + 2 * p + 1] = step_down(height, 2 * p + 1, x[:, width:])

        loop(layout[height][1] // 4, descend, 4)

    for c in range(chunks):
        near_copy(c).wait_recv()
    above = layout[1][2]

    def leaf_pair(p, x):
        y = step_down(0, p, x)
        far = jnp.concatenate(
            [mm(y[:, :width], basis[2 * p], NT), mm(y[:, width:], basis[2 * p + 1], NT)], axis=1
        )
        total = far + (near_own[p] + near_recv[p].astype(f32))
        out[:, pl.ds(pl.multiple_of(p * 2 * width, 2 * width), 2 * width)] = total.astype(bf16)

    def leaf_down(p):
        x = down[above + p]
        leaf_pair(2 * p, x[:, :width])
        leaf_pair(2 * p + 1, x[:, width:])

    loop(pairs // 2, leaf_down, 2)

    vec_send(1, 1).wait_send()

    @pl.when(sends_right)
    def _():
        for part in range(2):
            vec_send(0, part).wait_send()
            halo_send(0, part).wait_send()

    @pl.when(sends_left)
    def _():
        for part in range(2):
            vec_send(2, part).wait_send()
            halo_send(1, part).wait_send()

    for c in range(chunks):
        near_copy(c).wait_send()

    def end_sends(i, carry):
        root_copy(i).wait_send()
        top_copy(i).wait_send()
        return carry

    lax.fori_loop(1, n, end_sends, 0)


def shards(
    vectors, leaf_basis, local_transfer, coupling, coupling_source,
    top_transfer, top_coupling, top_target, top_source, near_blocks, near_source,
):
    n = lax.axis_size("leaf")
    rows = vectors.shape[0]
    leaves, width, rank = leaf_basis.shape
    nodes = local_transfer.shape[0]
    pairs = leaves // 2
    pair_total = leaves
    chunks = 4
    any_spec = pl.BlockSpec(memory_space=pl.ANY)
    smem = pl.BlockSpec(memory_space=pltpu.SMEM)
    vmem = pl.BlockSpec(memory_space=pltpu.VMEM)
    dma = pltpu.SemaphoreType.DMA
    return pl.pallas_call(
        functools.partial(kernel, n),
        out_shape=jax.ShapeDtypeStruct(vectors.shape, bf16),
        in_specs=[any_spec] * 5 + [smem] * 4 + [vmem] * 2,
        out_specs=vmem,
        scratch_shapes=[
            pltpu.VMEM((3, 2) + vectors.shape, bf16),
            pltpu.VMEM((3 * leaves, 2 * rows, width), bf16),
            pltpu.VMEM(leaf_basis.shape, bf16),
            pltpu.VMEM(local_transfer.shape, bf16),
            pltpu.VMEM(coupling.shape, bf16),
            pltpu.VMEM(near_blocks.shape, bf16),
            pltpu.VMEM((pair_total, rows, 2 * rank), bf16),
            pltpu.VMEM((2, pair_total, rows, 2 * rank), bf16),
            pltpu.VMEM((3 * nodes, rows, rank), bf16),
            pltpu.VMEM((pair_total, rows, 2 * rank), f32),
            pltpu.VMEM((pair_total, rows, 2 * rank), bf16),
            pltpu.VMEM((pairs, rows, 2 * width), f32),
            pltpu.VMEM((pairs, rows, 2 * width), bf16),
            pltpu.VMEM((pairs, rows, 2 * width), bf16),
            pltpu.VMEM((n, rows, rank), f32),
            pltpu.VMEM((n, rows, rank), bf16),
            pltpu.VMEM((n, rows, rank), f32),
            pltpu.VMEM((n, rows, rank), f32),
            dma((5,)),
            dma((3, 2)), dma((3, 2)),
            dma((2, 2)), dma((2, 2)),
            dma((chunks,)), dma((chunks,)),
            dma((n,)), dma((n,)),
            dma((n,)), dma((n,)),
        ],
        compiler_params=pltpu.CompilerParams(
            collective_id=0, has_side_effects=True, vmem_limit_bytes=56 * 1024 * 1024
        ),
    )(
        vectors, leaf_basis, local_transfer, coupling, near_blocks,
        coupling_source.T, near_source.T, top_target, top_source, top_transfer, top_coupling,
    )


def solution(mesh):
    placed = (
        P("rhs", "leaf"),
        P("leaf", None, None),
        P("leaf", None, None),
        P("leaf", None, None, None),
        P("leaf", None),
        P(),
        P("leaf", None, None),
        P("leaf"),
        P("leaf"),
        P("leaf", "rhs", None, None),
        P("leaf", "rhs"),
    )
    return jax.shard_map(
        shards, mesh=mesh, in_specs=placed, out_specs=P("rhs", "leaf"), check_vma=False
    )
```

time: 307 us -> 70.8 us (0.23)
  local copies, waits for them, and re-layouts: 127 us -> 20.6 us
  Pallas kernels: 0 us -> 48.9 us
  matrix products: 46.7 us -> 0 us
  starting transfers between devices: 42.8 us -> 0 us
  blocking collectives: 33 us -> 0 us
  other arithmetic: 26.4 us -> 0 us
  between operations: 15.4 us -> 0.01 us
  waiting for transfers between devices: 12.5 us -> 0 us
    pallas_call x0 -> x1, Pallas kernels: none -> 48.9 us  [shards(): pl.pallas_call(functools.partial(kernel, n), out_shape=jax.ShapeDtypeStru...]
    dot_general x29 -> x0, matrix products: 46.7 us -> none  [the longest x6 12 us: shards(): jnp.einsum('rtkm,tkmn->rtn', picked, coupling[couple_first_node:couple_fi...]
    ppermute x16 -> x0, starting transfers between devices: 42.8 us -> none  [the longest x8 32.4 us: padded(): before = lax.ppermute(last, axis, up)]
    slice x16 -> x0, local copies, waits for them, and re-layouts: 33.7 us -> none  [the longest x6 21.8 us: shards(): coupling[couple_first_node:couple_first_node + couple_node_count]]
    all_gather x2 -> x0, blocking collectives: 33 us -> none  [the longest x1 21.9 us: shards(): root_terms = lax.all_gather(root_term, 'leaf', axis=1, tiled=True)]
    unnamed x54 -> x3, local copies, waits for them, and re-layouts: 51 us -> 20.6 us
    gather x9 -> x0, local copies, waits for them, and re-layouts: 21.2 us -> none  [the longest x7 15.5 us: shards(): jnp.take(extended, source_ids.reshape(-1), axis=1)]
    concatenate x9 -> x0, other arithmetic: 13.7 us -> none  [the longest x8 13.6 us: padded(): array = jnp.concatenate([before, array, after], axis=dim)]
  transfers between devices with their start and end apart: 18 -> 0, of which waited for: 1 -> 0; matrix products, arithmetic and copies ran while one was open for 53% -> 0% of each run, Pallas kernels for 0% -> 0%
where the time goes in v1:
time: 70.8 us; the launch traced here: 69.6 us
  Pallas kernels  48.9 us (69%)
  local copies, waits for them, and re-layouts  20.6 us (29%)
    pallas_call x1, Pallas kernels, shards(): pl.pallas_call(functools.partial(kernel, n), out_shape=jax.ShapeDtypeStru...  48.9 us
    unnamed x3, local copies, waits for them, and re-layouts  20.6 us

profile of v1, /device:TPU:0, one launch (start us, length us, event | category | flops | bytes accessed | tf_op | source)
XLA Modules:
  0.0 69.6 jit_solution(17421297391965296368)
XLA Ops:
  0.0 5.0 %copy.12.trans_h = bf16[127,64,64]{2,1,0:T(8,128)(2,1)} copy(bf16[127,64,64]{0,2,1:T(8,128)(2,1)} %param.13) | data formatting | bytes 2080768 | tf_op args[2]
  5.0 13.9 %copy.13.coup_h = bf16[127,4,64,64]{3,2,1,0:T(8,128)(2,1)} copy(bf16[127,4,64,64]{0,3,2,1:T(8,128)(2,1)} %param.14) | data formatting | bytes 8323072 | tf_op args[3]
  19.0 48.9 %shard_map.109 = bf16[32,4096]{1,0:T(8,128)(2,1)} custom-call(bf16[32,4096]{1,0:T(8,128)(2,1)} %vec.1, bf16[64,64,64]{2,1,0:T(8,128)(2,1)} %basis_h.1, bf16[127,64,64]{2,1,0:T(8,128)(2,1)} %copy.12.trans_h, bf16[127,4,64,64]{3,2,1,0:T(8,128)(2,1)} %copy.13.coup_h, bf16[64,4,64,64]{3,2,1,0:T(8,128)(2,1)} %near_h.1, s32[4,127]{1,0:T(4,128)} %bitcast.2, ...), custom_call_target="tpu_custom_call" | custom-call | tf_op jit(solution)/shard_map/pallas_call | solution.py:466
  67.9 1.7 %copy.15 = bf16[32,4096]{1,0:T(8,128)(2,1)} copy(bf16[32,4096]{1,0:T(8,128)(2,1)} %shard_map.109) | data formatting | bytes 524288

commit v2 on v1

--- a/solution.py
+++ b/solution.py
@@ -56,7 +56,7 @@
     vec, basis_h, trans_h, coup_h, near_h,
     cs, ns, tt, ts, top_t, top_c,
     out,
-    vbuf, pts, basis, trans, coup, near,
+    vbuf, pts, basis, trans_raw, coup_raw, near, trans_rows, trans, coup,
     cp, halo, cl, field, down, near_own, near_send, near_recv,
     roots, uc, g, top_recv,
     local_sem, vs_sem, vr_sem, hs_sem, hr_sem, ns_sem, nr_sem, rs_sem, rr_sem, ts_sem, tr_sem,
@@ -67,7 +67,8 @@
     rows = vec.shape[0]
     layout = level_table(leaves)
     pairs = leaves // 2
-    slots = coup.shape[1]
+    slots = coup_raw.shape[0]
+    nodes = trans.shape[0]
     near_slots = near.shape[1]
     top_blocks = top_c.shape[0]
     me = lax.axis_index("leaf")
@@ -98,7 +99,7 @@
     local = [
         pltpu.make_async_copy(src, dst, local_sem.at[i])
         for i, (src, dst) in enumerate(
-            ((vec, vbuf.at[1, 0]), (basis_h, basis), (trans_h, trans), (near_h, near), (coup_h, coup))
+            ((vec, vbuf.at[1, 0]), (basis_h, basis), (trans_h, trans_raw), (near_h, near), (coup_h, coup_raw))
         )
     ]
     for copy in local:
@@ -142,6 +143,33 @@
         cp[pair_index] = jnp.concatenate([a, b], axis=1)
         cl[node_index] = a
         cl[node_index + 1] = b
+
+    def turned(a, b):
+        return jnp.concatenate([a, b], axis=0).astype(f32).T
+
+    def transfer_layout():
+        half = width // 2
+
+        def turn(m):
+            trans_rows[pl.ds(m, nodes, stride=half), :] = turned(trans_raw[m], trans_raw[m + half])
+
+        def split(t):
+            x = trans_rows[pl.ds(pl.multiple_of(t * half, half), half), :].astype(bf16)
+            trans[t, :half, :] = x[:, :width]
+            trans[t, half:, :] = x[:, width:]
+
+        loop(half, turn, 2)
+        lax.fori_loop(0, nodes // 8, lambda i, c: [split(8 * i + u) for u in range(8)] and c, 0)
+        for t in range(nodes // 8 * 8, nodes):
+            split(t)
+
+    def coupling_layout():
+        per = slots // 2
+        for k in range(per):
+            def turn(m):
+                coup[pl.ds(k * width + m, nodes, stride=per * width), :] = turned(coup_raw[k, m], coup_raw[k + per, m])
+
+            loop(width, turn, 2)
 
     def leaf_up(p):
         x = vbuf[1, 0, :, pl.ds(pl.multiple_of(p * 2 * width, 2 * width), 2 * width)]
@@ -161,6 +189,7 @@
         halo_send(1, 0).start()
 
     local[2].wait()
+    transfer_layout()
     for height in range(1, len(layout)):
         below_first, below_count, below_pair = layout[height - 1]
         first, count, pair = layout[height]
@@ -211,6 +240,9 @@
     @pl.when(sends_left)
     def _():
         halo_send(1, 1).start()
+
+    local[4].wait()
+    coupling_layout()
 
     def unpack_points(place, half):
         def body(p):
@@ -362,22 +394,33 @@
             else:
                 cl[base] = halo[place, pair][:, :width]
 
-    local[4].wait()
+    depth = slots // 2 * width
+    left_half = lax.broadcasted_iota(jnp.int32, (rows, 2 * width), 1) < width
     for first, count, pair in layout:
         base = 3 * first - (me - 1) * count
 
-        def node_field(t):
-            sources = [jnp.clip(base + cs[k, first + t], 0, cl.shape[0] - 1) for k in range(slots)]
-            x = jnp.concatenate([cl[source] for source in sources], axis=1)
-            return mm(x, coup[first + t].reshape(slots * width, width))
+        def node_terms(t):
+            c = [cl[jnp.clip(base + cs[k, first + t], 0, cl.shape[0] - 1)] for k in range(slots)]
+            per = slots // 2
+            x = jnp.concatenate(
+                [jnp.concatenate(c[:per], axis=1), jnp.concatenate(c[per:], axis=1)], axis=0
+            )
+            w = coup[pl.ds(pl.multiple_of((first + t) * depth, depth), depth), :].astype(bf16)
+            r = mm(x, w)
+            return r[:rows], r[rows:]
 
         if count > 1:
             def pair_field(p):
-                field[pair + p] = jnp.concatenate([node_field(2 * p), node_field(2 * p + 1)], axis=1)
+                a0, b0 = node_terms(2 * p)
+                a1, b1 = node_terms(2 * p + 1)
+                even = a0 + pltpu.roll(b0, width, 1)
+                odd = pltpu.roll(a1, width, 1) + b1
+                field[pair + p] = jnp.where(left_half, even, odd)
 
             loop(count // 2, pair_field, 4)
         else:
-            root_field = node_field(0)
+            a0, b0 = node_terms(0)
+            root_field = (a0 + pltpu.roll(b0, width, 1))[:, :width]
 
     def recv_top(i, total):
         top_wait(i).wait_recv()
@@ -456,6 +499,7 @@
     rows = vectors.shape[0]
     leaves, width, rank = leaf_basis.shape
     nodes = local_transfer.shape[0]
+    slots = coupling.shape[1]
     pairs = leaves // 2
     pair_total = leaves
     chunks = 4
@@ -472,9 +516,12 @@
             pltpu.VMEM((3, 2) + vectors.shape, bf16),
             pltpu.VMEM((3 * leaves, 2 * rows, width), bf16),
             pltpu.VMEM(leaf_basis.shape, bf16),
+            pltpu.VMEM((width, rank, nodes), bf16),
+            pltpu.VMEM((slots, rank, rank, nodes), bf16),
+            pltpu.VMEM(near_blocks.shape, bf16),
+            pltpu.VMEM((nodes * rank // 2, 2 * rank), f32),
             pltpu.VMEM(local_transfer.shape, bf16),
-            pltpu.VMEM(coupling.shape, bf16),
-            pltpu.VMEM(near_blocks.shape, bf16),
+            pltpu.VMEM((nodes * slots // 2 * rank, 2 * rank), f32),
             pltpu.VMEM((pair_total, rows, 2 * rank), bf16),
             pltpu.VMEM((2, pair_total, rows, 2 * rank), bf16),
             pltpu.VMEM((3 * nodes, rows, rank), bf16),
@@ -498,7 +545,7 @@
             collective_id=0, has_side_effects=True, vmem_limit_bytes=56 * 1024 * 1024
         ),
     )(
-        vectors, leaf_basis, local_transfer, coupling, near_blocks,
+        vectors, leaf_basis, local_transfer.transpose(1, 2, 0), coupling.transpose(1, 2, 3, 0), near_blocks,
         coupling_source.T, near_source.T, top_target, top_source, top_transfer, top_coupling,
     )
 

time: 70.8 us -> 55.2 us (0.78); the launches traced: 69.6 us -> 55.1 us
  local copies, waits for them, and re-layouts: 20.6 us -> 1.67 us
  Pallas kernels: 48.9 us -> 53.4 us
    unnamed x3 -> x1, local copies, waits for them, and re-layouts: 20.6 us -> 1.67 us
    pallas_call x1, Pallas kernels: 48.9 us -> 53.4 us  [shards(): pl.pallas_call(functools.partial(kernel, n), out_shape=jax.ShapeDtypeStru...]
where the time goes in v2:
time: 55.2 us; the launch traced here: 55.1 us
  Pallas kernels  53.4 us (97%)
  local copies, waits for them, and re-layouts  1.67 us (3%)
    pallas_call x1, Pallas kernels, shards(): pl.pallas_call(functools.partial(kernel, n), out_shape=jax.ShapeDtypeStru...  53.4 us
    unnamed x1, local copies, waits for them, and re-layouts  1.67 us

profile of v2, /device:TPU:0, one launch (start us, length us, event | category | flops | bytes accessed | tf_op | source)
XLA Modules:
  0.0 55.1 jit_solution(15406895142686308583)
XLA Ops:
  0.0 53.4 %shard_map.109 = bf16[32,4096]{1,0:T(8,128)(2,1)} custom-call(bf16[32,4096]{1,0:T(8,128)(2,1)} %vec.1, bf16[64,64,64]{2,1,0:T(8,128)(2,1)} %basis_h.1, bf16[64,64,127]{2,1,0:T(8,128)(2,1)} %bitcast.5, bf16[4,64,64,127]{3,2,1,0:T(8,128)(2,1)} %bitcast.4, bf16[64,4,64,64]{3,2,1,0:T(8,128)(2,1)} %near_h.1, s32[4,127]{1,0:T(4,128)} %bitcast.6, s32[4,64]{1,0:T(4,128)} %bitcast.7, ...), custom_call_target="tpu_custom_call" | custom-call | tf_op jit(solution)/shard_map/pallas_call | solution.py:510
  53.4 1.7 %copy.13 = bf16[32,4096]{1,0:T(8,128)(2,1)} copy(bf16[32,4096]{1,0:T(8,128)(2,1)} %shard_map.109) | data formatting | bytes 524288

commit v3 on v2

--- a/solution.py
+++ b/solution.py
@@ -75,6 +75,10 @@
     mine = lax.axis_index("rhs")
     other = 1 - mine
     has_left, has_right = me > 0, me < n - 1
+    odd = lax.rem(me, 2)
+    buddy = me + 1 - 2 * odd
+    far = me - 1 + 2 * odd
+    has_far = jnp.logical_and(far >= 0, far < n)
 
     def peer_of(i):
         return lax.rem(me + i, n)
@@ -88,30 +92,30 @@
     lax.fori_loop(1, n, greet, 0)
     pl.semaphore_signal(barrier, inc=1, device_id=(me, other), device_id_type=MESH)
 
-    @pl.when(has_left)
-    def _():
-        pl.semaphore_signal(barrier, inc=1, device_id=(me - 1, other), device_id_type=MESH)
-
-    @pl.when(has_right)
-    def _():
-        pl.semaphore_signal(barrier, inc=1, device_id=(me + 1, other), device_id_type=MESH)
-
     local = [
         pltpu.make_async_copy(src, dst, local_sem.at[i])
         for i, (src, dst) in enumerate(
-            ((vec, vbuf.at[1, 0]), (basis_h, basis), (trans_h, trans_raw), (near_h, near), (coup_h, coup_raw))
+            ((vec, vbuf.at[0, 0]), (basis_h, basis), (trans_h, trans_raw), (near_h, near), (coup_h, coup_raw))
         )
     ]
     for copy in local:
         copy.start()
 
-    pl.semaphore_wait(barrier, n + jnp.where(has_left, 1, 0) + jnp.where(has_right, 1, 0))
-
-    def vec_send(place, half):
-        target = (me + (1 - place), mine if half == 0 else other)
-        return pltpu.make_async_remote_copy(
-            src_ref=vec, dst_ref=vbuf.at[place, half],
-            send_sem=vs_sem.at[place, half], recv_sem=vr_sem.at[place, half],
+    pl.semaphore_wait(barrier, n)
+
+    def vec_send(kind, half):
+        source = vec
+        if half == 1 and kind > 0:
+            source = vbuf.at[0, 1] if kind == 1 else vbuf.at[2, 0]
+        if kind == 1:
+            target = (buddy, mine)
+        elif kind == 2 and half == 0:
+            target = (far, mine)
+        else:
+            target = (me, other)
+        return pltpu.make_async_remote_copy(
+            src_ref=source, dst_ref=vbuf.at[kind, half],
+            send_sem=vs_sem.at[kind, half], recv_sem=vr_sem.at[kind, half],
             device_id=target, device_id_type=MESH,
         )
 
@@ -124,17 +128,12 @@
         )
 
     sends_right, sends_left = has_right, has_left
-    vec_send(1, 1).start()
-
-    @pl.when(sends_right)
-    def _():
-        vec_send(0, 0).start()
-        vec_send(0, 1).start()
-
-    @pl.when(sends_left)
+    vec_send(0, 1).start()
+    vec_send(1, 0).start()
+
+    @pl.when(has_far)
     def _():
         vec_send(2, 0).start()
-        vec_send(2, 1).start()
 
     local[0].wait()
     local[1].wait()
@@ -172,7 +171,7 @@
             loop(width, turn, 2)
 
     def leaf_up(p):
-        x = vbuf[1, 0, :, pl.ds(pl.multiple_of(p * 2 * width, 2 * width), 2 * width)]
+        x = vbuf[0, 0, :, pl.ds(pl.multiple_of(p * 2 * width, 2 * width), 2 * width)]
         x0, x1 = x[:, :width], x[:, width:]
         c0 = mm(x0, basis[2 * p]).astype(bf16)
         c1 = mm(x1, basis[2 * p + 1]).astype(bf16)
@@ -241,44 +240,52 @@
     def _():
         halo_send(1, 1).start()
 
+    vec_send(0, 1).wait_recv()
+    vec_send(1, 1).start()
+
+    @pl.when(has_far)
+    def _():
+        vec_send(2, 0).wait_recv()
+        vec_send(2, 1).start()
+
     local[4].wait()
     coupling_layout()
 
-    def unpack_points(place, half):
+    def unpack_points(kind, half):
+        place = (1, 2 - 2 * odd, 2 * odd)[kind]
+
         def body(p):
-            x = vbuf[place, half, :, pl.ds(pl.multiple_of(p * 2 * width, 2 * width), 2 * width)]
+            x = vbuf[kind, half, :, pl.ds(pl.multiple_of(p * 2 * width, 2 * width), 2 * width)]
             pts[place * leaves + 2 * p, half * rows:(half + 1) * rows, :] = x[:, :width]
             pts[place * leaves + 2 * p + 1, half * rows:(half + 1) * rows, :] = x[:, width:]
 
         loop(pairs, body, 8)
 
+    @pl.when(jnp.logical_not(has_far))
+    def _():
+        vbuf[2] = jnp.zeros(vbuf.shape[1:], bf16)
+
+    @pl.when(jnp.logical_not(has_left))
+    def _():
+        halo[0] = jnp.zeros(halo.shape[1:], bf16)
+
+    @pl.when(jnp.logical_not(has_right))
+    def _():
+        halo[1] = jnp.zeros(halo.shape[1:], bf16)
+
+    unpack_points(0, 0)
+    unpack_points(0, 1)
+    vec_send(1, 0).wait_recv()
     unpack_points(1, 0)
-
-    @pl.when(jnp.logical_not(has_left))
-    def _():
-        vbuf[0] = jnp.zeros(vbuf.shape[1:], bf16)
-        halo[0] = jnp.zeros(halo.shape[1:], bf16)
-
-    @pl.when(jnp.logical_not(has_right))
-    def _():
-        vbuf[2] = jnp.zeros(vbuf.shape[1:], bf16)
-        halo[1] = jnp.zeros(halo.shape[1:], bf16)
-
+    unpack_points(2, 0)
     vec_send(1, 1).wait_recv()
     unpack_points(1, 1)
-    for half in range(2):
-        @pl.when(has_left)
-        def _():
-            vec_send(0, half).wait_recv()
-
-        unpack_points(0, half)
-
-        @pl.when(has_right)
-        def _():
-            vec_send(2, half).wait_recv()
-
-        unpack_points(2, half)
-
+
+    @pl.when(has_far)
+    def _():
+        vec_send(2, 1).wait_recv()
+
+    unpack_points(2, 1)
     local[3].wait()
     leaf_base = (me - 1) * leaves
 
@@ -414,8 +421,8 @@
                 a0, b0 = node_terms(2 * p)
                 a1, b1 = node_terms(2 * p + 1)
                 even = a0 + pltpu.roll(b0, width, 1)
-                odd = pltpu.roll(a1, width, 1) + b1
-                field[pair + p] = jnp.where(left_half, even, odd)
+                uneven = pltpu.roll(a1, width, 1) + b1
+                field[pair + p] = jnp.where(left_half, even, uneven)
 
             loop(count // 2, pair_field, 4)
         else:
@@ -466,19 +473,24 @@
 
     loop(pairs // 2, leaf_down, 2)
 
+    vec_send(0, 1).wait_send()
+    vec_send(1, 0).wait_send()
     vec_send(1, 1).wait_send()
 
+    @pl.when(has_far)
+    def _():
+        vec_send(2, 0).wait_send()
+        vec_send(2, 1).wait_send()
+
     @pl.when(sends_right)
     def _():
-        for part in range(2):
-            vec_send(0, part).wait_send()
-            halo_send(0, part).wait_send()
+        halo_send(0, 0).wait_send()
+        halo_send(0, 1).wait_send()
 
     @pl.when(sends_left)
     def _():
-        for part in range(2):
-            vec_send(2, part).wait_send()
-            halo_send(1, part).wait_send()
+        halo_send(1, 0).wait_send()
+        halo_send(1, 1).wait_send()
 
     for c in range(chunks):
         near_copy(c).wait_send()

time: 55.2 us -> 55.2 us (level)
  no operation moved by 1% of the time
where the time goes in v3:
time: 55.2 us; the launch traced here: 55.1 us
  Pallas kernels  53.4 us (97%)
  local copies, waits for them, and re-layouts  1.67 us (3%)
    pallas_call x1, Pallas kernels, shards(): pl.pallas_call(functools.partial(kernel, n), out_shape=jax.ShapeDtypeStru...  53.4 us
    unnamed x1, local copies, waits for them, and re-layouts  1.67 us

profile of v3, /device:TPU:0, one launch (start us, length us, event | category | flops | bytes accessed | tf_op | source)
XLA Modules:
  0.0 55.1 jit_solution(16937852828321567895)
XLA Ops:
  0.0 53.4 %shard_map.109 = bf16[32,4096]{1,0:T(8,128)(2,1)} custom-call(bf16[32,4096]{1,0:T(8,128)(2,1)} %vec.1, bf16[64,64,64]{2,1,0:T(8,128)(2,1)} %basis_h.1, bf16[64,64,127]{2,1,0:T(8,128)(2,1)} %bitcast.5, bf16[4,64,64,127]{3,2,1,0:T(8,128)(2,1)} %bitcast.4, bf16[64,4,64,64]{3,2,1,0:T(8,128)(2,1)} %near_h.1, s32[4,127]{1,0:T(4,128)} %bitcast.6, s32[4,64]{1,0:T(4,128)} %bitcast.7, ...), custom_call_target="tpu_custom_call" | custom-call | tf_op jit(solution)/shard_map/pallas_call | solution.py:522
  53.4 1.7 %copy.13 = bf16[32,4096]{1,0:T(8,128)(2,1)} copy(bf16[32,4096]{1,0:T(8,128)(2,1)} %shard_map.109) | data formatting | bytes 524288

commit v4 on v3

--- a/solution.py
+++ b/solution.py
@@ -41,8 +41,12 @@
         unroll -= 1
 
     def step(i, carry):
-        for u in range(unroll):
-            body(i * unroll + u)
+        parts = [body(i * unroll + u) for u in range(unroll)]
+        if hasattr(parts[0], "__next__"):
+            for part in parts:
+                next(part)
+            for part in parts:
+                next(part, None)
         return carry
 
     if count == unroll:
@@ -157,9 +161,10 @@
             trans[t, :half, :] = x[:, :width]
             trans[t, half:, :] = x[:, width:]
 
-        loop(half, turn, 2)
-        lax.fori_loop(0, nodes // 8, lambda i, c: [split(8 * i + u) for u in range(8)] and c, 0)
-        for t in range(nodes // 8 * 8, nodes):
+        loop(half, turn, 8)
+        whole = nodes // 16 * 16
+        loop(whole, split, 16)
+        for t in range(whole, nodes):
             split(t)
 
     def coupling_layout():
@@ -168,7 +173,7 @@
             def turn(m):
                 coup[pl.ds(k * width + m, nodes, stride=per * width), :] = turned(coup_raw[k, m], coup_raw[k + per, m])
 
-            loop(width, turn, 2)
+            loop(width, turn, 8)
 
     def leaf_up(p):
         x = vbuf[0, 0, :, pl.ds(pl.multiple_of(p * 2 * width, 2 * width), 2 * width)]
@@ -177,7 +182,7 @@
         c1 = mm(x1, basis[2 * p + 1]).astype(bf16)
         store_pair(p, leaves + 2 * p, c0, c1)
 
-    loop(pairs, leaf_up, 4)
+    loop(pairs, leaf_up, 16)
 
     @pl.when(sends_right)
     def _():
@@ -199,9 +204,11 @@
 
         if count > 1:
             def up(p):
-                store_pair(pair + p, 3 * first + count + 2 * p, lift(2 * p), lift(2 * p + 1))
-
-            loop(count // 2, up, 4)
+                a, b = lift(2 * p), lift(2 * p + 1)
+                yield
+                store_pair(pair + p, 3 * first + count + 2 * p, a, b)
+
+            loop(count // 2, up, 16)
         else:
             c = lift(0)
             cp[pair] = jnp.concatenate([c, c], axis=1)
@@ -259,7 +266,7 @@
             pts[place * leaves + 2 * p, half * rows:(half + 1) * rows, :] = x[:, :width]
             pts[place * leaves + 2 * p + 1, half * rows:(half + 1) * rows, :] = x[:, width:]
 
-        loop(pairs, body, 8)
+        loop(pairs, body, 16)
 
     @pl.when(jnp.logical_not(has_far))
     def _():
@@ -313,7 +320,7 @@
         )
 
     for c in range(chunks):
-        loop(chunk, lambda p: near_pair(c * chunk + p), 2)
+        loop(chunk, lambda p: near_pair(c * chunk + p), 4)
         near_copy(c).start()
 
     def recv_roots(i, carry):
@@ -330,9 +337,10 @@
         def upper_up(j):
             h = size + j
             x = mm(uc[2 * h], top_t[2 * h - 2]) + mm(uc[2 * h + 1], top_t[2 * h - 1])
+            yield
             uc[h] = x.astype(bf16)
 
-        loop(size, upper_up, 4)
+        loop(size, upper_up, 8)
         size //= 2
     terms = [mm(uc[ts[b]], top_c[b]) for b in range(top_blocks)]
 
@@ -344,17 +352,20 @@
             total = term if total is None else total + term
         g[h] = total
 
-    loop(n - 2, upper_gather, 2)
+    loop(n - 2, upper_gather, 16)
     size = 2
     while size < half_n:
         def upper_down(j):
             h = size + j
             w = top_t[pl.ds(2 * h - 2, 2)].reshape(2 * width, width)
             x = mm_split(g[h], w, NT)
-            g[2 * h] = g[2 * h] + x[:, :width]
-            g[2 * h + 1] = g[2 * h + 1] + x[:, width:]
-
-        loop(size, upper_down, 4)
+            even = g[2 * h] + x[:, :width]
+            uneven = g[2 * h + 1] + x[:, width:]
+            yield
+            g[2 * h] = even
+            g[2 * h + 1] = uneven
+
+        loop(size, upper_down, 8)
         size *= 2
 
     def top_copy(i):
@@ -397,7 +408,7 @@
                     cl[base + 2 * p] = x[:, :width]
                     cl[base + 2 * p + 1] = x[:, width:]
 
-                loop(count // 2, unpack, 8)
+                loop(count // 2, unpack, 16)
             else:
                 cl[base] = halo[place, pair][:, :width]
 
@@ -424,7 +435,7 @@
                 uneven = pltpu.roll(a1, width, 1) + b1
                 field[pair + p] = jnp.where(left_half, even, uneven)
 
-            loop(count // 2, pair_field, 4)
+            loop(count // 2, pair_field, 8)
         else:
             a0, b0 = node_terms(0)
             root_field = (a0 + pltpu.roll(b0, width, 1))[:, :width]
@@ -449,10 +460,13 @@
 
         def descend(p):
             x = down[above + p]
-            down[pair + 2 * p] = step_down(height, 2 * p, x[:, :width])
-            down[pair + 2 * p + 1] = step_down(height, 2 * p + 1, x[:, width:])
-
-        loop(layout[height][1] // 4, descend, 4)
+            even = step_down(height, 2 * p, x[:, :width])
+            uneven = step_down(height, 2 * p + 1, x[:, width:])
+            yield
+            down[pair + 2 * p] = even
+            down[pair + 2 * p + 1] = uneven
+
+        loop(layout[height][1] // 4, descend, 8)
 
     for c in range(chunks):
         near_copy(c).wait_recv()
@@ -471,7 +485,7 @@
         leaf_pair(2 * p, x[:, :width])
         leaf_pair(2 * p + 1, x[:, width:])
 
-    loop(pairs // 2, leaf_down, 2)
+    loop(pairs // 2, leaf_down, 8)
 
     vec_send(0, 1).wait_send()
     vec_send(1, 0).wait_send()

time: 55.2 us -> 45.1 us (0.82)
  Pallas kernels: 53.4 us -> 43.3 us
    pallas_call x1, Pallas kernels: 53.4 us -> 43.3 us  [shards(): pl.pallas_call(functools.partial(kernel, n), out_shape=jax.ShapeDtypeStru...]
where the time goes in v4:
time: 45.1 us; the launch traced here: 45 us
  Pallas kernels  43.3 us (96%)
  local copies, waits for them, and re-layouts  1.67 us (4%)
    pallas_call x1, Pallas kernels, shards(): pl.pallas_call(functools.partial(kernel, n), out_shape=jax.ShapeDtypeStru...  43.3 us
    unnamed x1, local copies, waits for them, and re-layouts  1.67 us

profile of v4, /device:TPU:0, one launch (start us, length us, event | category | flops | bytes accessed | tf_op | source)
XLA Modules:
  0.0 45.0 jit_solution(1910510819122527280)
XLA Ops:
  0.0 43.3 %shard_map.109 = bf16[32,4096]{1,0:T(8,128)(2,1)} custom-call(bf16[32,4096]{1,0:T(8,128)(2,1)} %vec.1, bf16[64,64,64]{2,1,0:T(8,128)(2,1)} %basis_h.1, bf16[64,64,127]{2,1,0:T(8,128)(2,1)} %bitcast.5, bf16[4,64,64,127]{3,2,1,0:T(8,128)(2,1)} %bitcast.4, bf16[64,4,64,64]{3,2,1,0:T(8,128)(2,1)} %near_h.1, s32[4,127]{1,0:T(4,128)} %bitcast.6, s32[4,64]{1,0:T(4,128)} %bitcast.7, ...), custom_call_target="tpu_custom_call" | custom-call | tf_op jit(solution)/shard_map/pallas_call | solution.py:536
  43.3 1.7 %copy.13 = bf16[32,4096]{1,0:T(8,128)(2,1)} copy(bf16[32,4096]{1,0:T(8,128)(2,1)} %shard_map.109) | data formatting | bytes 524288

commit v5 on v4

--- a/solution.py
+++ b/solution.py
@@ -102,10 +102,9 @@
             ((vec, vbuf.at[0, 0]), (basis_h, basis), (trans_h, trans_raw), (near_h, near), (coup_h, coup_raw))
         )
     ]
-    for copy in local:
-        copy.start()
-
-    pl.semaphore_wait(barrier, n)
+    for i in (0, 1, 2, 4):
+        local[i].start()
+
 
     def vec_send(kind, half):
         source = vec
@@ -132,13 +131,6 @@
         )
 
     sends_right, sends_left = has_right, has_left
-    vec_send(0, 1).start()
-    vec_send(1, 0).start()
-
-    @pl.when(has_far)
-    def _():
-        vec_send(2, 0).start()
-
     local[0].wait()
     local[1].wait()
 
@@ -148,16 +140,17 @@
         cl[node_index + 1] = b
 
     def turned(a, b):
-        return jnp.concatenate([a, b], axis=0).astype(f32).T
+        return jnp.concatenate([a, b], axis=0).T.astype(f32)
 
     def transfer_layout():
         half = width // 2
+        pitch = half + 8
 
         def turn(m):
-            trans_rows[pl.ds(m, nodes, stride=half), :] = turned(trans_raw[m], trans_raw[m + half])
+            trans_rows[pl.ds(m, nodes, stride=pitch), :] = turned(trans_raw[m], trans_raw[m + half])
 
         def split(t):
-            x = trans_rows[pl.ds(pl.multiple_of(t * half, half), half), :].astype(bf16)
+            x = trans_rows[pl.ds(pl.multiple_of(t * pitch, 8), half), :].astype(bf16)
             trans[t, :half, :] = x[:, :width]
             trans[t, half:, :] = x[:, width:]
 
@@ -171,7 +164,7 @@
         per = slots // 2
         for k in range(per):
             def turn(m):
-                coup[pl.ds(k * width + m, nodes, stride=per * width), :] = turned(coup_raw[k, m], coup_raw[k + per, m])
+                coup[pl.ds(k * width + m, nodes, stride=per * width + 8), :] = turned(coup_raw[k, m], coup_raw[k + per, m])
 
             loop(width, turn, 8)
 
@@ -183,6 +176,15 @@
         store_pair(p, leaves + 2 * p, c0, c1)
 
     loop(pairs, leaf_up, 16)
+    local[3].start()
+    pl.semaphore_wait(barrier, n)
+    vec_send(0, 1).start()
+    vec_send(1, 0).start()
+
+    @pl.when(has_far)
+    def _():
+        vec_send(2, 0).start()
+
 
     @pl.when(sends_right)
     def _():
@@ -220,17 +222,15 @@
 
     def root_copy(i):
         return pltpu.make_async_remote_copy(
-            src_ref=roots.at[me], dst_ref=roots.at[me],
-            send_sem=rs_sem.at[i], recv_sem=rr_sem.at[me],
+            src_ref=roots.at[me], dst_ref=roots.at[me], send_sem=rs_sem, recv_sem=rr_sem,
             device_id=(peer_of(i), mine), device_id_type=MESH,
         )
 
-    def root_recv(i):
-        source = peer_of(i)
+    def all_peers(buffer, send_sem, recv_sem):
+        part = buffer.at[pl.ds(0, n - 1)]
         return pltpu.make_async_remote_copy(
-            src_ref=roots.at[source], dst_ref=roots.at[source],
-            send_sem=rs_sem.at[i], recv_sem=rr_sem.at[source],
-            device_id=(source, mine), device_id_type=MESH,
+            src_ref=part, dst_ref=part, send_sem=send_sem, recv_sem=recv_sem,
+            device_id=(peer_of(1), mine), device_id_type=MESH,
         )
 
     def send_roots(i, carry):
@@ -297,11 +297,9 @@
     leaf_base = (me - 1) * leaves
 
     def near_leaf(i):
-        total = None
-        for j in range(near_slots):
-            term = mm(pts[jnp.clip(ns[j, i] - leaf_base, 0, 3 * leaves - 1)], near[i, j], NT)
-            total = term if total is None else total + term
-        return total
+        x = [pts[jnp.clip(ns[j, i] - leaf_base, 0, 3 * leaves - 1)] for j in range(near_slots)]
+        blocks = [near[i, j] for j in range(near_slots)]
+        return mm(jnp.concatenate(x, axis=1), jnp.concatenate(blocks, axis=1), NT)
 
     def near_pair(p):
         both = jnp.concatenate([near_leaf(2 * p), near_leaf(2 * p + 1)], axis=1)
@@ -323,11 +321,7 @@
         loop(chunk, lambda p: near_pair(c * chunk + p), 4)
         near_copy(c).start()
 
-    def recv_roots(i, carry):
-        root_recv(i).wait_recv()
-        return carry
-
-    lax.fori_loop(1, n, recv_roots, 0)
+    all_peers(roots, rs_sem, rr_sem).wait_recv()
     half_n = n // 2
     uc[0] = jnp.zeros(uc.shape[1:], bf16)
     uc[1] = jnp.zeros(uc.shape[1:], bf16)
@@ -368,20 +362,13 @@
         loop(size, upper_down, 8)
         size *= 2
 
+    top_recv[me] = g[half_n + me // 2]
+
     def top_copy(i):
         peer = peer_of(i)
         return pltpu.make_async_remote_copy(
-            src_ref=g.at[half_n + peer // 2], dst_ref=top_recv.at[me],
-            send_sem=ts_sem.at[i], recv_sem=tr_sem.at[me],
+            src_ref=g.at[half_n + peer // 2], dst_ref=top_recv.at[me], send_sem=ts_sem, recv_sem=tr_sem,
             device_id=(peer, mine), device_id_type=MESH,
-        )
-
-    def top_wait(i):
-        source = peer_of(i)
-        return pltpu.make_async_remote_copy(
-            src_ref=g.at[half_n + source // 2], dst_ref=top_recv.at[source],
-            send_sem=ts_sem.at[i], recv_sem=tr_sem.at[source],
-            device_id=(source, mine), device_id_type=MESH,
         )
 
     def send_top(i, carry):
@@ -423,7 +410,7 @@
             x = jnp.concatenate(
                 [jnp.concatenate(c[:per], axis=1), jnp.concatenate(c[per:], axis=1)], axis=0
             )
-            w = coup[pl.ds(pl.multiple_of((first + t) * depth, depth), depth), :].astype(bf16)
+            w = coup[pl.ds(pl.multiple_of((first + t) * (depth + 8), 8), depth), :].astype(bf16)
             r = mm(x, w)
             return r[:rows], r[rows:]
 
@@ -440,11 +427,10 @@
             a0, b0 = node_terms(0)
             root_field = (a0 + pltpu.roll(b0, width, 1))[:, :width]
 
-    def recv_top(i, total):
-        top_wait(i).wait_recv()
-        return total + top_recv[peer_of(i)]
-
-    parent = lax.fori_loop(1, n, recv_top, g[half_n + me // 2])
+    all_peers(top_recv, ts_sem, tr_sem).wait_recv()
+    parent = top_recv[0]
+    for i in range(1, n):
+        parent = parent + top_recv[i]
     root_down = (root_field + mm_split(parent, trans[root_row], NT)).astype(bf16)
 
     def step_down(height, q, x):
@@ -509,12 +495,8 @@
     for c in range(chunks):
         near_copy(c).wait_send()
 
-    def end_sends(i, carry):
-        root_copy(i).wait_send()
-        top_copy(i).wait_send()
-        return carry
-
-    lax.fori_loop(1, n, end_sends, 0)
+    all_peers(roots, rs_sem, rr_sem).wait_send()
+    all_peers(top_recv, ts_sem, tr_sem).wait_send()
 
 
 def shards(
@@ -545,9 +527,9 @@
             pltpu.VMEM((width, rank, nodes), bf16),
             pltpu.VMEM((slots, rank, rank, nodes), bf16),
             pltpu.VMEM(near_blocks.shape, bf16),
-            pltpu.VMEM((nodes * rank // 2, 2 * rank), f32),
+            pltpu.VMEM((nodes * (rank // 2 + 8), 2 * rank), f32),
             pltpu.VMEM(local_transfer.shape, bf16),
-            pltpu.VMEM((nodes * slots // 2 * rank, 2 * rank), f32),
+            pltpu.VMEM((nodes * (slots // 2 * rank + 8), 2 * rank), f32),
             pltpu.VMEM((pair_total, rows, 2 * rank), bf16),
             pltpu.VMEM((2, pair_total, rows, 2 * rank), bf16),
             pltpu.VMEM((3 * nodes, rows, rank), bf16),
@@ -564,8 +546,7 @@
             dma((3, 2)), dma((3, 2)),
             dma((2, 2)), dma((2, 2)),
             dma((chunks,)), dma((chunks,)),
-            dma((n,)), dma((n,)),
-            dma((n,)), dma((n,)),
+            dma, dma, dma, dma,
         ],
         compiler_params=pltpu.CompilerParams(
             collective_id=0, has_side_effects=True, vmem_limit_bytes=56 * 1024 * 1024

time: 45.1 us -> 42.3 us (0.938)
  Pallas kernels: 43.3 us -> 40.4 us
    pallas_call x1, Pallas kernels: 43.3 us -> 40.4 us  [shards(): pl.pallas_call(functools.partial(kernel, n), out_shape=jax.ShapeDtypeStru...]
where the time goes in v5:
time: 42.3 us; the launch traced here: 42.1 us
  Pallas kernels  40.4 us (96%)
  local copies, waits for them, and re-layouts  1.67 us (4%)
    pallas_call x1, Pallas kernels, shards(): pl.pallas_call(functools.partial(kernel, n), out_shape=jax.ShapeDtypeStru...  40.4 us
    unnamed x1, local copies, waits for them, and re-layouts  1.67 us

profile of v5, /device:TPU:0, one launch (start us, length us, event | category | flops | bytes accessed | tf_op | source)
XLA Modules:
  0.0 42.1 jit_solution(18265538621167850797)
XLA Ops:
  0.0 40.4 %shard_map.109 = bf16[32,4096]{1,0:T(8,128)(2,1)} custom-call(bf16[32,4096]{1,0:T(8,128)(2,1)} %vec.1, bf16[64,64,64]{2,1,0:T(8,128)(2,1)} %basis_h.1, bf16[64,64,127]{2,1,0:T(8,128)(2,1)} %bitcast.5, bf16[4,64,64,127]{3,2,1,0:T(8,128)(2,1)} %bitcast.4, bf16[64,4,64,64]{3,2,1,0:T(8,128)(2,1)} %near_h.1, s32[4,127]{1,0:T(4,128)} %bitcast.6, s32[4,64]{1,0:T(4,128)} %bitcast.7, ...), custom_call_target="tpu_custom_call" | custom-call | tf_op jit(solution)/shard_map/pallas_call | solution.py:518
  40.4 1.7 %copy.13 = bf16[32,4096]{1,0:T(8,128)(2,1)} copy(bf16[32,4096]{1,0:T(8,128)(2,1)} %shard_map.109) | data formatting | bytes 524288

commit v6 on v5

--- a/solution.py
+++ b/solution.py
@@ -102,7 +102,7 @@
             ((vec, vbuf.at[0, 0]), (basis_h, basis), (trans_h, trans_raw), (near_h, near), (coup_h, coup_raw))
         )
     ]
-    for i in (0, 1, 2, 4):
+    for i in (0, 1, 2):
         local[i].start()
 
 
@@ -133,6 +133,7 @@
     sends_right, sends_left = has_right, has_left
     local[0].wait()
     local[1].wait()
+    local[4].start()
 
     def store_pair(pair_index, node_index, a, b):
         cp[pair_index] = jnp.concatenate([a, b], axis=1)
@@ -160,13 +161,10 @@
         for t in range(whole, nodes):
             split(t)
 
-    def coupling_layout():
-        per = slots // 2
-        for k in range(per):
-            def turn(m):
-                coup[pl.ds(k * width + m, nodes, stride=per * width + 8), :] = turned(coup_raw[k, m], coup_raw[k + per, m])
-
-            loop(width, turn, 8)
+    per = slots // 2
+
+    def turn_coupling(k, m):
+        coup[pl.ds(k * width + m, nodes, stride=per * width + 8), :] = turned(coup_raw[k, m], coup_raw[k + per, m])
 
     def leaf_up(p):
         x = vbuf[0, 0, :, pl.ds(pl.multiple_of(p * 2 * width, 2 * width), 2 * width)]
@@ -196,6 +194,8 @@
 
     local[2].wait()
     transfer_layout()
+    local[4].wait()
+    early = 8
     for height in range(1, len(layout)):
         below_first, below_count, below_pair = layout[height - 1]
         first, count, pair = layout[height]
@@ -215,6 +215,8 @@
             c = lift(0)
             cp[pair] = jnp.concatenate([c, c], axis=1)
             cl[3 * first + count] = c
+        for m in range(early * (height - 1), early * height):
+            turn_coupling(0, m)
     root_row = layout[-1][0]
     root_pair = layout[-1][2]
     root_term = mm(cp[root_pair][:, :width], trans[root_row])
@@ -255,8 +257,10 @@
         vec_send(2, 0).wait_recv()
         vec_send(2, 1).start()
 
-    local[4].wait()
-    coupling_layout()
+    turns_done = early * (len(layout) - 1)
+    loop(width - turns_done, lambda m: turn_coupling(0, turns_done + m), 8)
+    for k in range(1, per):
+        loop(width, lambda m: turn_coupling(k, m), 8)
 
     def unpack_points(kind, half):
         place = (1, 2 - 2 * odd, 2 * odd)[kind]
@@ -317,9 +321,16 @@
             device_id=(me, other), device_id_type=MESH,
         )
 
-    for c in range(chunks):
+    for c in range(chunks - 1):
         loop(chunk, lambda p: near_pair(c * chunk + p), 4)
         near_copy(c).start()
+
+    rest = list(range((chunks - 1) * chunk, pairs))
+
+    def near_rest(count):
+        for p in rest[:count]:
+            near_pair(p)
+        del rest[:count]
 
     all_peers(roots, rs_sem, rr_sem).wait_recv()
     half_n = n // 2
@@ -335,8 +346,10 @@
             uc[h] = x.astype(bf16)
 
         loop(size, upper_up, 8)
+        near_rest(2)
         size //= 2
     terms = [mm(uc[ts[b]], top_c[b]) for b in range(top_blocks)]
+    near_rest(2)
 
     def upper_gather(j):
         h = j + 2
@@ -360,8 +373,11 @@
             g[2 * h + 1] = uneven
 
         loop(size, upper_down, 8)
+        near_rest(1)
         size *= 2
 
+    near_rest(len(rest))
+    near_copy(chunks - 1).start()
     top_recv[me] = g[half_n + me // 2]
 
     def top_copy(i):
@@ -401,31 +417,29 @@
 
     depth = slots // 2 * width
     left_half = lax.broadcasted_iota(jnp.int32, (rows, 2 * width), 1) < width
-    for first, count, pair in layout:
+
+    def node_terms(height, t):
+        first, count, _ = layout[height]
         base = 3 * first - (me - 1) * count
-
-        def node_terms(t):
-            c = [cl[jnp.clip(base + cs[k, first + t], 0, cl.shape[0] - 1)] for k in range(slots)]
-            per = slots // 2
-            x = jnp.concatenate(
-                [jnp.concatenate(c[:per], axis=1), jnp.concatenate(c[per:], axis=1)], axis=0
-            )
-            w = coup[pl.ds(pl.multiple_of((first + t) * (depth + 8), 8), depth), :].astype(bf16)
-            r = mm(x, w)
-            return r[:rows], r[rows:]
-
-        if count > 1:
-            def pair_field(p):
-                a0, b0 = node_terms(2 * p)
-                a1, b1 = node_terms(2 * p + 1)
-                even = a0 + pltpu.roll(b0, width, 1)
-                uneven = pltpu.roll(a1, width, 1) + b1
-                field[pair + p] = jnp.where(left_half, even, uneven)
-
-            loop(count // 2, pair_field, 8)
-        else:
-            a0, b0 = node_terms(0)
-            root_field = (a0 + pltpu.roll(b0, width, 1))[:, :width]
+        c = [cl[jnp.clip(base + cs[k, first + t], 0, cl.shape[0] - 1)] for k in range(slots)]
+        x = jnp.concatenate(
+            [jnp.concatenate(c[:per], axis=1), jnp.concatenate(c[per:], axis=1)], axis=0
+        )
+        w = coup[pl.ds(pl.multiple_of((first + t) * (depth + 8), 8), depth), :].astype(bf16)
+        r = mm(x, w)
+        return r[:rows], r[rows:]
+
+    def pair_field(height, p):
+        a0, b0 = node_terms(height, 2 * p)
+        a1, b1 = node_terms(height, 2 * p + 1)
+        even = a0 + pltpu.roll(b0, width, 1)
+        uneven = pltpu.roll(a1, width, 1) + b1
+        field[layout[height][2] + p] = jnp.where(left_half, even, uneven)
+
+    a0, b0 = node_terms(len(layout) - 1, 0)
+    root_field = (a0 + pltpu.roll(b0, width, 1))[:, :width]
+    for height in range(len(layout) - 2, 0, -1):
+        loop(layout[height][1] // 2, lambda p: pair_field(height, p), 16)
 
     all_peers(top_recv, ts_sem, tr_sem).wait_recv()
     parent = top_recv[0]
@@ -440,6 +454,7 @@
 
     top_height = len(layout) - 2
     down[layout[top_height][2]] = step_down(top_height, 0, root_down)
+    share = pairs // (len(layout) + 1)
     for height in range(top_height - 1, 0, -1):
         pair = layout[height][2]
         above = layout[height + 1][2]
@@ -453,6 +468,10 @@
             down[pair + 2 * p + 1] = uneven
 
         loop(layout[height][1] // 4, descend, 8)
+        for p in range(share * (top_height - 1 - height), share * (top_height - height)):
+            pair_field(0, p)
+    fields_done = share * (top_height - 1)
+    loop(pairs - fields_done, lambda p: pair_field(0, fields_done + p), 8)
 
     for c in range(chunks):
         near_copy(c).wait_recv()

time: 42.3 us -> 42.3 us (level)
  no operation moved by 1% of the time
where the time goes in v6:
time: 42.3 us; the launch traced here: 42.2 us
  Pallas kernels  40.5 us (96%)
  local copies, waits for them, and re-layouts  1.67 us (4%)
    pallas_call x1, Pallas kernels, shards(): pl.pallas_call(functools.partial(kernel, n), out_shape=jax.ShapeDtypeStru...  40.5 us
    unnamed x1, local copies, waits for them, and re-layouts  1.67 us

profile of v6, /device:TPU:0, one launch (start us, length us, event | category | flops | bytes accessed | tf_op | source)
XLA Modules:
  0.0 42.2 jit_solution(4419670522302276425)
XLA Ops:
  0.0 40.5 %shard_map.109 = bf16[32,4096]{1,0:T(8,128)(2,1)} custom-call(bf16[32,4096]{1,0:T(8,128)(2,1)} %vec.1, bf16[64,64,64]{2,1,0:T(8,128)(2,1)} %basis_h.1, bf16[64,64,127]{2,1,0:T(8,128)(2,1)} %bitcast.5, bf16[4,64,64,127]{3,2,1,0:T(8,128)(2,1)} %bitcast.4, bf16[64,4,64,64]{3,2,1,0:T(8,128)(2,1)} %near_h.1, s32[4,127]{1,0:T(4,128)} %bitcast.6, s32[4,64]{1,0:T(4,128)} %bitcast.7, ...), custom_call_target="tpu_custom_call" | custom-call | tf_op jit(solution)/shard_map/pallas_call | solution.py:537
  40.5 1.7 %copy.13 = bf16[32,4096]{1,0:T(8,128)(2,1)} copy(bf16[32,4096]{1,0:T(8,128)(2,1)} %shard_map.109) | data formatting | bytes 524288

commit v7 on v6

--- a/solution.py
+++ b/solution.py
@@ -131,6 +131,15 @@
         )
 
     sends_right, sends_left = has_right, has_left
+    pl.semaphore_wait(barrier, n)
+
+    @pl.when(has_far)
+    def _():
+        vec_send(2, 0).start()
+
+    vec_send(0, 1).start()
+    vec_send(1, 0).start()
+
     local[0].wait()
     local[1].wait()
     local[4].start()
@@ -175,14 +184,6 @@
 
     loop(pairs, leaf_up, 16)
     local[3].start()
-    pl.semaphore_wait(barrier, n)
-    vec_send(0, 1).start()
-    vec_send(1, 0).start()
-
-    @pl.when(has_far)
-    def _():
-        vec_send(2, 0).start()
-
 
     @pl.when(sends_right)
     def _():
@@ -195,7 +196,7 @@
     local[2].wait()
     transfer_layout()
     local[4].wait()
-    early = 8
+    early = 4
     for height in range(1, len(layout)):
         below_first, below_count, below_pair = layout[height - 1]
         first, count, pair = layout[height]

time: 42.3 us -> 42.6 us (level)
  no operation moved by 1% of the time
where the time goes in v7:
time: 42.6 us; the launch traced here: 42.4 us
  Pallas kernels  40.8 us (96%)
  local copies, waits for them, and re-layouts  1.67 us (4%)
    pallas_call x1, Pallas kernels, shards(): pl.pallas_call(functools.partial(kernel, n), out_shape=jax.ShapeDtypeStru...  40.8 us
    unnamed x1, local copies, waits for them, and re-layouts  1.67 us

profile of v7, /device:TPU:0, one launch (start us, length us, event | category | flops | bytes accessed | tf_op | source)
XLA Modules:
  0.0 42.4 jit_solution(14647122690400843714)
XLA Ops:
  0.0 40.8 %shard_map.109 = bf16[32,4096]{1,0:T(8,128)(2,1)} custom-call(bf16[32,4096]{1,0:T(8,128)(2,1)} %vec.1, bf16[64,64,64]{2,1,0:T(8,128)(2,1)} %basis_h.1, bf16[64,64,127]{2,1,0:T(8,128)(2,1)} %bitcast.5, bf16[4,64,64,127]{3,2,1,0:T(8,128)(2,1)} %bitcast.4, bf16[64,4,64,64]{3,2,1,0:T(8,128)(2,1)} %near_h.1, s32[4,127]{1,0:T(4,128)} %bitcast.6, s32[4,64]{1,0:T(4,128)} %bitcast.7, ...), custom_call_target="tpu_custom_call" | custom-call | tf_op jit(solution)/shard_map/pallas_call | solution.py:538
  40.8 1.7 %copy.13 = bf16[32,4096]{1,0:T(8,128)(2,1)} copy(bf16[32,4096]{1,0:T(8,128)(2,1)} %shard_map.109) | data formatting | bytes 524288

commit v8 on v7

--- a/solution.py
+++ b/solution.py
@@ -62,7 +62,7 @@
     out,
     vbuf, pts, basis, trans_raw, coup_raw, near, trans_rows, trans, coup,
     cp, halo, cl, field, down, near_own, near_send, near_recv,
-    roots, uc, g, top_recv,
+    roots, uc, g, top_recv, top_send,
     local_sem, vs_sem, vr_sem, hs_sem, hr_sem, ns_sem, nr_sem, rs_sem, rr_sem, ts_sem, tr_sem,
 ):
     n = roots_n
@@ -221,7 +221,14 @@
     root_row = layout[-1][0]
     root_pair = layout[-1][2]
     root_term = mm(cp[root_pair][:, :width], trans[root_row])
-    roots[me] = root_term
+
+    def fold(x):
+        return jnp.concatenate([x[:rows // 2], x[rows // 2:]], axis=1)
+
+    def unfold(x):
+        return jnp.concatenate([x[:, :width], x[:, width:]], axis=0)
+
+    roots[me] = fold(root_term)
 
     def root_copy(i):
         return pltpu.make_async_remote_copy(
@@ -337,7 +344,7 @@
     half_n = n // 2
     uc[0] = jnp.zeros(uc.shape[1:], bf16)
     uc[1] = jnp.zeros(uc.shape[1:], bf16)
-    loop(half_n, lambda j: uc.__setitem__(half_n + j, (roots[2 * j] + roots[2 * j + 1]).astype(bf16)), 4)
+    loop(half_n, lambda j: uc.__setitem__(half_n + j, unfold(roots[2 * j] + roots[2 * j + 1]).astype(bf16)), 4)
     size = half_n // 2
     while size >= 2:
         def upper_up(j):
@@ -379,12 +386,13 @@
 
     near_rest(len(rest))
     near_copy(chunks - 1).start()
-    top_recv[me] = g[half_n + me // 2]
+    loop(half_n, lambda j: top_send.__setitem__(j, fold(g[half_n + j])), 8)
+    top_recv[me] = top_send[me // 2]
 
     def top_copy(i):
         peer = peer_of(i)
         return pltpu.make_async_remote_copy(
-            src_ref=g.at[half_n + peer // 2], dst_ref=top_recv.at[me], send_sem=ts_sem, recv_sem=tr_sem,
+            src_ref=top_send.at[peer // 2], dst_ref=top_recv.at[me], send_sem=ts_sem, recv_sem=tr_sem,
             device_id=(peer, mine), device_id_type=MESH,
         )
 
@@ -442,10 +450,15 @@
     for height in range(len(layout) - 2, 0, -1):
         loop(layout[height][1] // 2, lambda p: pair_field(height, p), 16)
 
+    share = pairs // (len(layout) + 1)
+    fields_done = share * (len(layout) - 3)
+    loop(pairs - fields_done, lambda p: pair_field(0, fields_done + p), 16)
+
     all_peers(top_recv, ts_sem, tr_sem).wait_recv()
     parent = top_recv[0]
     for i in range(1, n):
         parent = parent + top_recv[i]
+    parent = unfold(parent)
     root_down = (root_field + mm_split(parent, trans[root_row], NT)).astype(bf16)
 
     def step_down(height, q, x):
@@ -455,7 +468,6 @@
 
     top_height = len(layout) - 2
     down[layout[top_height][2]] = step_down(top_height, 0, root_down)
-    share = pairs // (len(layout) + 1)
     for height in range(top_height - 1, 0, -1):
         pair = layout[height][2]
         above = layout[height + 1][2]
@@ -471,8 +483,6 @@
         loop(layout[height][1] // 4, descend, 8)
         for p in range(share * (top_height - 1 - height), share * (top_height - height)):
             pair_field(0, p)
-    fields_done = share * (top_height - 1)
-    loop(pairs - fields_done, lambda p: pair_field(0, fields_done + p), 8)
 
     for c in range(chunks):
         near_copy(c).wait_recv()
@@ -558,10 +568,11 @@
             pltpu.VMEM((pairs, rows, 2 * width), f32),
             pltpu.VMEM((pairs, rows, 2 * width), bf16),
             pltpu.VMEM((pairs, rows, 2 * width), bf16),
-            pltpu.VMEM((n, rows, rank), f32),
+            pltpu.VMEM((n, rows // 2, 2 * rank), f32),
             pltpu.VMEM((n, rows, rank), bf16),
             pltpu.VMEM((n, rows, rank), f32),
-            pltpu.VMEM((n, rows, rank), f32),
+            pltpu.VMEM((n, rows // 2, 2 * rank), f32),
+            pltpu.VMEM((n // 2, rows // 2, 2 * rank), f32),
             dma((5,)),
             dma((3, 2)), dma((3, 2)),
             dma((2, 2)), dma((2, 2)),

time: 42.6 us -> 41.3 us (0.969)
  Pallas kernels: 40.8 us -> 39.5 us
    pallas_call x1, Pallas kernels: 40.8 us -> 39.5 us  [shards(): pl.pallas_call(functools.partial(kernel, n), out_shape=jax.ShapeDtypeStru...]
where the time goes in v8:
time: 41.3 us; the launch traced here: 41.2 us
  Pallas kernels  39.5 us (96%)
  local copies, waits for them, and re-layouts  1.67 us (4%)
    pallas_call x1, Pallas kernels, shards(): pl.pallas_call(functools.partial(kernel, n), out_shape=jax.ShapeDtypeStru...  39.5 us
    unnamed x1, local copies, waits for them, and re-layouts  1.67 us

profile of v8, /device:TPU:0, one launch (start us, length us, event | category | flops | bytes accessed | tf_op | source)
XLA Modules:
  0.0 41.2 jit_solution(15905961061629027427)
XLA Ops:
  0.0 39.5 %shard_map.109 = bf16[32,4096]{1,0:T(8,128)(2,1)} custom-call(bf16[32,4096]{1,0:T(8,128)(2,1)} %vec.1, bf16[64,64,64]{2,1,0:T(8,128)(2,1)} %basis_h.1, bf16[64,64,127]{2,1,0:T(8,128)(2,1)} %bitcast.5, bf16[4,64,64,127]{3,2,1,0:T(8,128)(2,1)} %bitcast.4, bf16[64,4,64,64]{3,2,1,0:T(8,128)(2,1)} %near_h.1, s32[4,127]{1,0:T(4,128)} %bitcast.6, s32[4,64]{1,0:T(4,128)} %bitcast.7, ...), custom_call_target="tpu_custom_call" | custom-call | tf_op jit(solution)/shard_map/pallas_call | solution.py:548
  39.5 1.7 %copy.13 = bf16[32,4096]{1,0:T(8,128)(2,1)} copy(bf16[32,4096]{1,0:T(8,128)(2,1)} %shard_map.109) | data formatting | bytes 524288
